TPU v7x, 32 devices: a whole 2x2x4 slice. The times are simulated.
32 devices in a mesh: ctx: 8 (over y, x, core), tp: 4 (over z).
Axes of the slice: x: 2, y: 2, z: 4, core: 2. Of those that a mesh axis runs over, the one named last changes fastest.
Arguments:
- query: bfloat16 [2048, 5120], P('ctx', 'tp'), may hold values from -6 to 6
- key_projected: bfloat16 [2048, 1024], P('ctx', 'tp'), may hold values from -6 to 6
- value: bfloat16 [2048, 1024], P('ctx', 'tp'), may hold values from -6 to 6
- attention_output: bfloat16 [2048, 5120], P('ctx', 'tp'), may hold values from -6 to 6
- output_gradient: bfloat16 [2048, 5120], P('ctx', 'tp'), may hold values from -6 to 6
- lse: float32 [40, 2048], P('tp', 'ctx'), may hold values from 4 to 7
- block_mask: int32 [16, 16], replicated, may hold values from 0 to 1, as said below
- positions: int32 [2048], P('ctx'), may hold values from 0 to 1023, as said below
- segments: int32 [2048], replicated, may hold values from 0 to 31, as said below
- w_query: bfloat16 [5120, 5120], P(None, 'tp'), may hold values from -0.078125 to 0.078125
- key_weight: bfloat16 [5120, 1024], P(None, 'tp'), may hold values from -0.078125 to 0.078125
- value_weight: bfloat16 [5120, 1024], P(None, 'tp'), may hold values from -0.078125 to 0.078125
Outputs:
- input_grad_t: bfloat16 [5120, 2048], P('tp', 'ctx')
Inputs may be any that keep to these rules, and one draw needn't show every extreme that they name: block_mask[a, b] is 1 exactly when tile b is tile a or an ancestor of tile a in a forest of tiles in which every tile's parent is an earlier tile. `positions`: a token's position is 128 times its tile's number of ancestors plus its offset from the first token of its segment within the tile. `segments`: never falling along the tokens; one segment a tile, except that a tile that is no other tile's ancestor may hold two, the second beginning inside it.
All inputs are finite; a program needn't handle non-finite values.
Results may differ from a plain program's by a relative error of at most 0.0065.
The roundings to bfloat16 on the way count: a program that leaves them out, or rounds other values in their place, can miss the bound.
Values may be sent and summed in bfloat16 or wider, within the bound.
A program may use at most 128 MiB of HBM per device.

v0:
```python
import jax
import jax.numpy as jnp
from jax import lax
from jax.sharding import PartitionSpec as P

QUERY_HEADS = 40
KEY_VALUE_HEADS = 8
HEAD_SIZE = 128
TILE = 128


rope_base = 1000000.0


def rope_tables(positions, head_dim):
    half = head_dim // 2
    exponent = jnp.arange(half).astype(jnp.float32) * (2.0 / head_dim)
    inverse = jnp.power(jnp.float32(rope_base), -exponent)
    angles = positions.astype(jnp.float32)[:, None] * inverse[None, :]
    cosine_table = jnp.cos(angles)
    sine_table = jnp.sin(angles)
    return (
        jnp.concatenate([cosine_table, cosine_table], 1),
        jnp.concatenate([sine_table, sine_table], 1),
    )


def rotate_forward(values, cosine_table, sine_table):
    half = values.shape[-1] // 2
    turned = jnp.concatenate([-values[..., half:], values[..., :half]], -1)
    return values * cosine_table[:, None, :] + turned * sine_table[:, None, :]


def unrotate_halves(grads, cosine_table, sine_table):
    half = grads.shape[-1] // 2
    scaled = grads * sine_table[:, None, :]
    turned = jnp.concatenate([scaled[..., half:], -scaled[..., :half]], -1)
    return grads * cosine_table[:, None, :] + turned


def block_size(tile):
    for multiple in (4, 2, 1):
        return multiple * tile
    return tile


def pair_mask(block_mask, segments, q_start, q_count, k_start, k_count, tile):
    q_start = jnp.asarray(q_start)
    k_start = jnp.asarray(k_start)
    table = lax.dynamic_slice(
        block_mask, (q_start // tile, k_start // tile), (q_count // tile, k_count // tile)
    )
    needed = jnp.any(table > 0)
    wide = (
        jnp.broadcast_to(
            table[:, None, :, None], (q_count // tile, tile, k_count // tile, tile)
        ).reshape(q_count, k_count)
        > 0
    )
    q_index = q_start + jnp.arange(q_count)
    k_index = k_start + jnp.arange(k_count)
    seg_query = lax.dynamic_slice_in_dim(segments, q_start, q_count)
    seg_key = lax.dynamic_slice_in_dim(segments, k_start, k_count)
    same_tile = q_index[:, None] // tile == k_index[None, :] // tile
    inner = (k_index[None, :] <= q_index[:, None]) & (seg_query[:, None] == seg_key[None, :])
    return (wide & (jnp.logical_not(same_tile) | inner), needed)


def score_grads(query_blk, grad_blk, lse_blk, delta_blk, key_blk, value_blk, allowed, logit_scale):
    scores = (
        jnp.einsum("tkgd,skd->tkgs", query_blk, key_blk, preferred_element_type=jnp.float32)
        * logit_scale
    )
    probs = jnp.where(allowed[:, None, None, :], jnp.exp(scores - lse_blk[..., None]), 0.0)
    dprobs = jnp.einsum("tkgd,skd->tkgs", grad_blk, value_blk, preferred_element_type=jnp.float32)
    dscore = probs * (dprobs - delta_blk[..., None])
    return (probs.astype(jnp.bfloat16), dscore.astype(jnp.bfloat16))


def local(
    query,
    key_projected,
    value,
    attention_output,
    output_gradient,
    lse,
    block_mask,
    positions,
    segments,
    w_query,
    key_weight,
    value_weight,
):
    tok_rows = query.shape[0]
    kv_local = key_projected.shape[1] // HEAD_SIZE
    query_groups = QUERY_HEADS // KEY_VALUE_HEADS
    heads_local = kv_local * query_groups
    logit_scale = HEAD_SIZE ** (-0.5)
    q_start = lax.axis_index("ctx") * tok_rows
    cosine_table, sine_table = rope_tables(positions, HEAD_SIZE)
    query_rotated = rotate_forward(
        query.astype(jnp.float32).reshape(tok_rows, heads_local, HEAD_SIZE),
        cosine_table,
        sine_table,
    ).astype(jnp.bfloat16)
    query_four = query_rotated.reshape(tok_rows, kv_local, query_groups, HEAD_SIZE)
    key_rotated = rotate_forward(
        key_projected.astype(jnp.float32).reshape(tok_rows, kv_local, HEAD_SIZE),
        cosine_table,
        sine_table,
    ).astype(jnp.bfloat16)
    grad_four = output_gradient.reshape(tok_rows, kv_local, query_groups, HEAD_SIZE)
    row_dot_delta = jnp.sum(
        grad_four.astype(jnp.float32)
        * attention_output.reshape(tok_rows, kv_local, query_groups, HEAD_SIZE).astype(jnp.float32),
        -1,
    )
    row_logsumexp = lse.T.reshape(tok_rows, kv_local, query_groups)
    key_whole, value_whole = (
        lax.all_gather(
            key_rotated.reshape(tok_rows, kv_local * HEAD_SIZE), "ctx", axis=0, tiled=True
        ),
        lax.all_gather(value, "ctx", axis=0, tiled=True),
    )
    key_total = key_whole.shape[0]
    key_step = block_size(TILE)
    query_empty = jnp.zeros((tok_rows, kv_local, query_groups, HEAD_SIZE), jnp.float32)

    def all_terms(accum, index):
        k_start = index * key_step
        key_blk = lax.dynamic_slice_in_dim(key_whole, k_start, key_step, 0).reshape(
            key_step, kv_local, HEAD_SIZE
        )
        value_blk = lax.dynamic_slice_in_dim(value_whole, k_start, key_step, 0).reshape(
            key_step, kv_local, HEAD_SIZE
        )
        allowed, needed = pair_mask(
            block_mask, segments, q_start, tok_rows, k_start, key_step, TILE
        )
        probs_bf, dscore_bf = score_grads(
            query_four,
            grad_four,
            row_logsumexp,
            row_dot_delta,
            key_blk,
            value_blk,
            allowed,
            logit_scale,
        )
        query_sum = accum + jnp.einsum(
            "tkgs,skd->tkgd", dscore_bf, key_blk, preferred_element_type=jnp.float32
        )
        key_part = jnp.einsum(
            "tkgs,tkgd->skd", dscore_bf, query_four, preferred_element_type=jnp.float32
        )
        value_part = jnp.einsum(
            "tkgs,tkgd->skd", probs_bf, grad_four, preferred_element_type=jnp.float32
        )
        stacked = jnp.concatenate(
            [
                key_part.reshape(key_step, kv_local * HEAD_SIZE),
                value_part.reshape(key_step, kv_local * HEAD_SIZE),
            ],
            1,
        )
        return (query_sum, stacked)

    query_acc, blocks = lax.scan(all_terms, query_empty, jnp.arange(key_total // key_step))
    terms = blocks.reshape(key_total, 2 * kv_local * HEAD_SIZE)
    summed = lax.psum_scatter(terms, "ctx", scatter_dimension=0, tiled=True)
    key_rot_grad = (
        summed[:, : kv_local * HEAD_SIZE].reshape(tok_rows, kv_local, HEAD_SIZE) * logit_scale
    )
    value_gradient = summed[:, kv_local * HEAD_SIZE :].reshape(tok_rows, kv_local, HEAD_SIZE)
    query_rot_grad = (query_acc * logit_scale).reshape(tok_rows, heads_local, HEAD_SIZE)
    query_grad = (
        unrotate_halves(query_rot_grad, cosine_table, sine_table)
        .astype(jnp.bfloat16)
        .reshape(tok_rows, heads_local * HEAD_SIZE)
    )
    key_gradient = (
        unrotate_halves(key_rot_grad, cosine_table, sine_table)
        .astype(jnp.bfloat16)
        .reshape(tok_rows, kv_local * HEAD_SIZE)
    )
    value_grad_bf = value_gradient.astype(jnp.bfloat16).reshape(tok_rows, kv_local * HEAD_SIZE)
    contract = (((1,), (1,)), ((), ()))
    result = lax.dot_general(w_query, query_grad, contract, preferred_element_type=jnp.float32)
    result = result + lax.dot_general(
        key_weight, key_gradient, contract, preferred_element_type=jnp.float32
    )
    result = result + lax.dot_general(
        value_weight, value_grad_bf, contract, preferred_element_type=jnp.float32
    )
    return lax.psum_scatter(result, "tp", scatter_dimension=0, tiled=True).astype(jnp.bfloat16)


def solution(mesh):
    in_specs = (
        P("ctx", "tp"),
        P("ctx", "tp"),
        P("ctx", "tp"),
        P("ctx", "tp"),
        P("ctx", "tp"),
        P("tp", "ctx"),
        P(),
        P("ctx"),
        P(),
        P(None, "tp"),
        P(None, "tp"),
        P(None, "tp"),
    )
    out_specs = P("tp", "ctx")
    return jax.shard_map(local, mesh=mesh, in_specs=in_specs, out_specs=out_specs, check_vma=False)
```

profile of v0, /device:TPU:12, one launch (start us, length us, event | category | flops | bytes accessed | tf_op | source)
XLA Modules:
  0.0 295.6 jit_solution(5583087504961671691)
XLA Ops:
  6.5 1.8 copy.40
  12.7 1.3 copy.39
  14.0 1.2 convert_element_type.64
  15.2 1.3 copy.41
  16.6 2.6 copy.42
  20.1 2.1 multiply_reduce_fusion
  22.6 11.3 %all-gather.5.cloned.1.call-done = bf16[2048,256]{0,1:T(8,128)(2,1)} async-done(((bf16[256,256]{0,1:T(8,128)(2,1)}), bf16[2048,256]{0,1:T(8,128)(2,1)}) %all-gather.5.cloned.1.call-update) | async-done | bytes 1048592 | tf_op jit(solution)/shard_map/all_gather | solution.py:123
  33.8 25.5 %all-gather.3.cloned.1.call-done = bf16[2048,256]{0,1:T(8,128)(2,1)} async-done(((bf16[256,256]{0,1:T(8,128)(2,1)}), bf16[2048,256]{0,1:T(8,128)(2,1)}) %all-gather.3.cloned.1.call-update) | async-done | bytes 1048592 | tf_op jit(solution)/shard_map/all_gather | solution.py:120
  59.3 70.1 %while.17 = (s32[]{:T(128)}, f32[256,2,5,128]{0,3,2,1:T(8,128)}, f32[4,512,512]{2,1,0:T(8,128)}, s32[4]{0:T(128)S(1)}, bf16[2048,256]{0,1:T(8,128)(2,1)}, /*inde...) while((s32[]{:T(128)}, f32[256,2,5,128]{0,3,2,1:T(8,128)}, ...), condition=%wide.wide.region_2.3_spmd.clone, body=%wide.wide.region_1.2_spmd.clone.sunk | while | flops 1692676096 | bytes 52168356 | solution.py:168
  62.8 1.1 constant_dynamic-slice_fusion.4
  65.0 1.2 fusion.83
  66.2 1.6 fusion.81
  69.9 1.1 copy-done.2
  71.0 1.1 maximum_bitcast_fusion.3
  72.0 2.5 copy.80
  74.6 2.3 constant_dynamic-update-slice_fusion.3
  80.3 1.1 constant_dynamic-slice_fusion.4
  82.5 1.2 fusion.83
  83.7 1.6 fusion.81
  87.4 1.1 copy-done.2
  88.5 1.1 maximum_bitcast_fusion.3
  89.5 2.5 copy.80
  92.1 2.2 constant_dynamic-update-slice_fusion.3
  97.8 1.1 constant_dynamic-slice_fusion.4
  100.0 1.2 fusion.83
  101.2 1.6 fusion.81
  104.9 1.1 copy-done.2
  105.9 1.1 maximum_bitcast_fusion.3
  107.0 2.5 copy.80
  109.5 2.4 constant_dynamic-update-slice_fusion.3
  115.4 1.1 constant_dynamic-slice_fusion.4
  117.6 1.2 fusion.83
  118.8 1.6 fusion.81
  122.5 1.1 copy-done.2
  123.5 1.1 maximum_bitcast_fusion.3
  124.6 2.5 copy.80
  127.1 2.3 constant_dynamic-update-slice_fusion.3
  131.2 1.4 broadcast_multiply_fusion
  133.9 16.1 %fusion.26 = f32[256,5120]{1,0:T(8,128)} fusion(bf16[256,1280]{0,1:T(8,128)(2,1)S(1)} %fusion.17, bf16[5120,1280]{1,0:T(8,128)(2,1)} %param.23), kind=kOutput, calls=%fused_computation.72 | convolution fusion | flops 3355443200 | bytes 19005440 | tf_op jit(solution)/shard_map/dot_general | solution.py:188
  150.1 31.0 %reduce-scatter.3.cloned.1.call-done = f32[256,512]{1,0:T(8,128)} async-done(((f32[2048,512]{1,0:T(8,128)}), f32[256,512]{1,0:T(8,128)}) %reduce-scatter.3.cloned.1.call-update) | async-done | bytes 524304 | tf_op jit(solution)/shard_map/reduce_scatter | solution.py:170
  181.1 1.7 slice.47
  182.8 1.1 reshape.260
  183.9 1.0 broadcast_multiply_fusion.1
  185.8 3.5 %convolution_add_fusion.1 = f32[256,5120]{1,0:T(8,128)S(1)} fusion(f32[256,5120]{1,0:T(8,128)} %fusion.26, bf16[5120,256]{1,0:T(8,128)(2,1)S(1)} %copy-done, f32[32,8,2,128]{3,2,1,0:T(2,128)S(1)} %bitcast.191, f32[32,8,2,128]{3,2,1,0:T(2,128)S(1)} %bitcast.192, f32[256,512]{1,0:T(8,128)S(1)} %copy-done.11), kind=kOutput, calls=%fused_computation.34 | convolution fusion | flops 672595968 | bytes 13893632 | tf_op jit(solution)/shard_map/dot_general | solution.py:189
  189.4 3.2 %fusion.14 = f32[5120,256]{0,1:T(8,128)} fusion(f32[256,5120]{1,0:T(8,128)S(1)} %convolution_add_fusion.1, bf16[5120,256]{1,0:T(8,128)(2,1)S(1)} %copy-done.4, f32[256,512]{1,0:T(8,128)S(1)} %copy-done.11), kind=kOutput, calls=%fused_computation.35 | convolution fusion | flops 672399360 | bytes 13238272 | tf_op jit(solution)/shard_map/dot_general | solution.py:192
  192.6 94.0 %reduce-scatter.5.cloned.1.call-done = f32[1280,256]{0,1:T(8,128)} async-done(((f32[5120,256]{0,1:T(8,128)}), f32[1280,256]{0,1:T(8,128)}) %reduce-scatter.5.cloned.1.call-update) | async-done | bytes 1310736 | tf_op jit(solution)/shard_map/reduce_scatter | solution.py:195
  286.6 1.4 convert_element_type.71
  288.0 1.1 copy.46
  (138 shorter events, 33.0 us)
Async XLA Ops:
  6.5 179.3 %copy-start = (bf16[5120,256]{1,0:T(8,128)(2,1)S(1)}, bf16[5120,256]{1,0:T(8,128)(2,1)}, u32[]{:S(2)}) copy-start(bf16[5120,256]{1,0:T(8,128)(2,1)} %param.24) | copy-start | bytes 7864324
  6.5 5.6 %copy-start.15 = (f32[10,256]{1,0:T(8,128)S(1)}, f32[10,256]{1,0:T(8,128)}, u32[]{:S(2)}) copy-start(f32[10,256]{1,0:T(8,128)} %param.19) | copy-start | bytes 30724
  6.5 27.3 %all-gather.5.cloned.1.call-start = ((), (), s32[]{:S(2)}) async-start(), calls=%async_computation.3 | async-start | bytes 1179648 | tf_op jit(solution)/shard_map/all_gather | solution.py:123
  8.4 51.0 %all-gather.3.cloned.1.call-start = ((), (), s32[]{:S(2)}) async-start(), calls=%async_computation.2 | async-start | bytes 1179648 | tf_op jit(solution)/shard_map/all_gather | solution.py:120
  11.2 11.0 %copy-start.7 = (f32[256,128]{0,1:T(8,128)}, f32[256,128]{0,1:T(8,128)S(1)}, u32[]{:S(2)}) copy-start(f32[256,128]{0,1:T(8,128)S(1)} %get-tuple-element.400) | copy-start | bytes 393220
  11.2 11.0 %copy-start.9 = (f32[256,128]{0,1:T(8,128)}, f32[256,128]{0,1:T(8,128)S(1)}, u32[]{:S(2)}) copy-start(f32[256,128]{0,1:T(8,128)S(1)} %get-tuple-element.397) | copy-start | bytes 393220
  12.0 169.1 %reduce-scatter.3.cloned.1.call-start = ((), (), s32[]{:S(2)}) async-start(), calls=%async_computation.4 | async-start | bytes 4718592 | tf_op jit(solution)/shard_map/reduce_scatter | solution.py:170
  16.5 5.7 %copy-start.5 = (bf16[256,1280]{0,1:T(8,128)(2,1)}, bf16[256,1280]{0,1:T(8,128)(2,1)S(1)}, u32[]{:S(2)}) copy-start(bf16[256,1280]{0,1:T(8,128)(2,1)S(1)} %copy.41) | copy-start | bytes 1966084
  19.2 2.9 copy-start.3
  63.9 1.1 copy-start.6
  63.9 1.1 copy-start.16
  65.0 1.2 copy-start.14
  67.9 1.3 copy-start.1
  69.9 1.1 copy-start.2
  81.4 1.1 copy-start.6
  81.4 1.1 copy-start.16
  82.5 1.2 copy-start.14
  85.4 1.3 copy-start.1
  87.4 1.1 copy-start.2
  98.9 1.1 copy-start.6
  98.9 1.1 copy-start.16
  100.0 1.2 copy-start.14
  102.8 1.3 copy-start.1
  104.9 1.1 copy-start.2
  116.5 1.1 copy-start.6
  116.5 1.1 copy-start.16
  117.6 1.2 copy-start.14
  120.4 1.3 copy-start.1
  122.5 1.1 copy-start.2
  129.5 0.9 copy-start.13
  129.5 1.6 copy-start.12
  129.5 3.2 %copy-start.10 = (f32[256,128]{0,1:T(8,128)S(1)}, f32[256,128]{0,1:T(8,128)}, u32[]{:S(2)}) copy-start(f32[256,128]{0,1:T(8,128)} %copy-done.9) | copy-start | bytes 393220
  129.5 157.1 %reduce-scatter.5.cloned.1.call-start = ((), (), s32[]{:S(2)}) async-start(), calls=%async_computation.5 | async-start | bytes 6553600 | tf_op jit(solution)/shard_map/reduce_scatter | solution.py:195
  132.8 0.9 copy-start.8
  181.1 4.7 %copy-start.11 = (f32[256,512]{1,0:T(8,128)S(1)}, f32[256,512]{1,0:T(8,128)}, u32[]{:S(2)}) copy-start(f32[256,512]{1,0:T(8,128)} %reduce-scatter.3.cloned.1.call-done) | copy-start | bytes 1572868
  185.8 3.6 %copy-start.4 = (bf16[5120,256]{1,0:T(8,128)(2,1)S(1)}, bf16[5120,256]{1,0:T(8,128)(2,1)}, u32[]{:S(2)}) copy-start(bf16[5120,256]{1,0:T(8,128)(2,1)} %param.25) | copy-start | bytes 7864324
Sparse Core Ops, SparseCore 0:
  9.2 24.5 all-gather.4
  35.7 23.5 all-gather.2
  129.6 51.4 reduce-scatter.2
  192.7 93.8 reduce-scatter.4
where the time goes:
time: 299 us; the launch traced here: 296 us
  waiting for transfers between devices  162 us (54%)
  local copies, waits for them, and re-layouts  52.9 us (18%)
  matrix products  44.3 us (15%)
  other arithmetic  19.8 us (7%)
  between operations  13.4 us (4%)
  loops' own time  3 us (1%)
    reduce_scatter x1, waiting for transfers between devices, local(): lax.psum_scatter(result, 'tp', scatter_dimension=0, tiled=True)  94 us
    reduce_scatter x1, waiting for transfers between devices, local(): summed = lax.psum_scatter(terms, 'ctx', scatter_dimension=0, tiled=True)  31 us
    all_gather x1, waiting for transfers between devices, local(): lax.all_gather(key_rotated.reshape(tok_rows, kv_local * HEAD_SIZE), 'ctx'...  25.5 us
    dynamic_update_slice x8, local copies, waits for them, and re-layouts, local(): lax.scan(all_terms, query_empty, jnp.arange(key_total // key_step))  19.4 us
    dot_general x1, matrix products, local(): lax.dot_general(w_query, query_grad, contract, preferred_element_type=jnp...  16.1 us
    all_gather x1, waiting for transfers between devices, local(): lax.all_gather(value, 'ctx', axis=0, tiled=True)  11.3 us
    unnamed x28, local copies, waits for them, and re-layouts  6.79 us
    dot_general x4, matrix products, score_grads(): jnp.einsum('tkgd,skd->tkgs', grad_blk, value_blk, preferred_element_type=...  6.47 us
  transfers between devices with their start and end apart: 4, of which 4 were waited for; matrix products, arithmetic and copies ran while one was open for 11% of the time, Pallas kernels for 0%

commit v1 on v0

v1 whole, which is shorter than its diff:
```python
import functools

import jax
import jax.numpy as jnp
from jax import lax
from jax.experimental import pallas as pl
from jax.experimental.pallas import tpu as pltpu
from jax.sharding import PartitionSpec as P

QUERY_HEADS = 40
KEY_VALUE_HEADS = 8
HEAD_SIZE = 128
TILE = 128
GROUP = QUERY_HEADS // KEY_VALUE_HEADS
SCALE = HEAD_SIZE ** (-0.5)
MESH = pl.DeviceIdType.MESH
VMEM_BYTES = 56 * 1024 * 1024

rope_base = 1000000.0


def rope_tables(positions, head_dim):
    half = head_dim // 2
    exponent = jnp.arange(half).astype(jnp.float32) * (2.0 / head_dim)
    inverse = jnp.power(jnp.float32(rope_base), -exponent)
    angles = positions.astype(jnp.float32)[:, None] * inverse[None, :]
    cosine_table = jnp.cos(angles)
    sine_table = jnp.sin(angles)
    return (
        jnp.concatenate([cosine_table, cosine_table], 1),
        jnp.concatenate([-sine_table, sine_table], 1),
    )


def swap_halves(x):
    half = HEAD_SIZE // 2
    return jnp.concatenate([x[..., half:], x[..., :half]], -1)


def dot(a, b, dims=((1,), (0,))):
    return lax.dot_general(a, b, (dims, ((), ())), preferred_element_type=jnp.float32)


def attention_kernel(
    start_ref, mask_ref, q_ref, do_ref, lse_ref, delta_ref, cos_ref, sin_ref, kv_ref, segq_ref, segk_ref,
    dq_ref, dkv_ref, qs, dos, qt_s, dot_s, lse_s, delta_s, dqt,
):
    tokens = q_ref.shape[0]
    kv_local = kv_ref.shape[1] // (2 * HEAD_SIZE)
    q_tiles = tokens // TILE
    wide = GROUP * TILE
    first_tile = start_ref[0]
    dkv_ref[...] = jnp.zeros_like(dkv_ref)
    dqt[...] = jnp.zeros_like(dqt)
    for t in range(q_tiles):
        rows = slice(t * TILE, (t + 1) * TILE)
        cosine = cos_ref[rows, :]
        sine = sin_ref[rows, :]
        for h in range(kv_local * GROUP):
            c, g = h // GROUP, h % GROUP
            part = slice(g * TILE, (g + 1) * TILE)
            cols = slice(h * HEAD_SIZE, (h + 1) * HEAD_SIZE)
            x = q_ref[rows, cols].astype(jnp.float32)
            x = x * cosine + pltpu.roll(x, HEAD_SIZE // 2, 1) * sine
            xb = x.astype(jnp.bfloat16)
            qs[t, c, part, :] = xb
            qt_s[t, c, :, part] = xb.astype(jnp.float32).T.astype(jnp.bfloat16)
            y = do_ref[rows, cols]
            dos[t, c, part, :] = y
            dot_s[t, c, :, part] = y.astype(jnp.float32).T.astype(jnp.bfloat16)
            lse_s[t, c, :, part] = lse_ref[h : h + 1, rows]
            delta_s[t, c, :, part] = delta_ref[h : h + 1, rows]

    def pair(t, k_tile, allowed):
        k_rows = pl.ds(pl.multiple_of(k_tile * TILE, TILE), TILE)
        for c in range(kv_local):
            key_cols = slice(c * HEAD_SIZE, (c + 1) * HEAD_SIZE)
            val_cols = slice((kv_local + c) * HEAD_SIZE, (kv_local + c + 1) * HEAD_SIZE)
            k = kv_ref[k_rows, key_cols]
            v = kv_ref[k_rows, val_cols]
            scores = dot(k, qt_s[t, c]) * SCALE
            probs = jnp.exp(scores - lse_s[t, c])
            if allowed is not None:
                probs = jnp.where(allowed, probs, 0.0)
            dscore = probs * (dot(v, dot_s[t, c]) - delta_s[t, c])
            pb = probs.astype(jnp.bfloat16)
            db = dscore.astype(jnp.bfloat16)
            dkv_ref[k_rows, key_cols] += dot(db, qs[t, c])
            dkv_ref[k_rows, val_cols] += dot(pb, dos[t, c])
            kt = k.astype(jnp.float32).T.astype(jnp.bfloat16)
            dqt[t, c] += dot(kt, db)

    for t in range(q_tiles):
        own = first_tile + t

        @pl.loop(0, own)
        def _(k_tile):
            @pl.when(mask_ref[own, k_tile] > 0)
            def _():
                pair(t, k_tile, None)

        row = lax.broadcasted_iota(jnp.int32, (TILE, TILE), 0)
        col = lax.broadcasted_iota(jnp.int32, (TILE, TILE), 1)
        seg_k = segk_ref[t * TILE : (t + 1) * TILE, :]
        seg_q = segq_ref[:, t * TILE : (t + 1) * TILE]
        inner = jnp.where((row <= col) & (seg_k == seg_q), 1.0, 0.0)
        inner = jnp.concatenate([inner] * GROUP, 1) > 0.5
        pair(t, own, inner)

        rows = slice(t * TILE, (t + 1) * TILE)
        cosine = cos_ref[rows, :]
        sine = sin_ref[rows, :]
        for h in range(kv_local * GROUP):
            c, g = h // GROUP, h % GROUP
            x = (dqt[t, c, :, g * TILE : (g + 1) * TILE] * SCALE).T
            x = x * cosine - pltpu.roll(x, HEAD_SIZE // 2, 1) * sine
            dq_ref[rows, h * HEAD_SIZE : (h + 1) * HEAD_SIZE] = x.astype(jnp.bfloat16)


def attention(first_tile, block_mask, query, grad, lse, delta, cosine, sine, kv_whole, seg_row):
    tokens = query.shape[0]
    kv_local = kv_whole.shape[1] // (2 * HEAD_SIZE)
    q_tiles = tokens // TILE
    wide = GROUP * TILE
    vm = pl.BlockSpec(memory_space=pltpu.VMEM)
    sm = pl.BlockSpec(memory_space=pltpu.SMEM)
    return pl.pallas_call(
        attention_kernel,
        out_shape=(
            jax.ShapeDtypeStruct(query.shape, jnp.bfloat16),
            jax.ShapeDtypeStruct(kv_whole.shape, jnp.float32),
        ),
        in_specs=[sm, sm] + [vm] * 9,
        out_specs=(vm, vm),
        scratch_shapes=[
            pltpu.VMEM((q_tiles, kv_local, wide, HEAD_SIZE), jnp.bfloat16),
            pltpu.VMEM((q_tiles, kv_local, wide, HEAD_SIZE), jnp.bfloat16),
            pltpu.VMEM((q_tiles, kv_local, HEAD_SIZE, wide), jnp.bfloat16),
            pltpu.VMEM((q_tiles, kv_local, HEAD_SIZE, wide), jnp.bfloat16),
            pltpu.VMEM((q_tiles, kv_local, 1, wide), jnp.float32),
            pltpu.VMEM((q_tiles, kv_local, 1, wide), jnp.float32),
            pltpu.VMEM((q_tiles, kv_local, HEAD_SIZE, wide), jnp.float32),
        ],
        compiler_params=pltpu.CompilerParams(vmem_limit_bytes=VMEM_BYTES),
        name="attention",
    )(first_tile, block_mask, query, grad, lse, delta, cosine, sine, kv_whole, seg_row, seg_row.reshape(tokens, 1))


def project_kernel(
    n, dq_ref, dkv_ref, wq_ref, wk_ref, wv_ref, out_ref,
    wq, wk, wv, acc, send, send_scale, recv, recv_scale,
    w_sem, send_sem, recv_sem, send_scale_sem, recv_scale_sem,
):
    me = lax.axis_index("tp")
    chunk_rows = out_ref.shape[0]
    sub_rows = acc.shape[0]
    subs = chunk_rows // sub_rows
    steps = 2 * (n - 1) * subs

    def plan(i):
        way = lax.rem(i, 2)
        rightward = jnp.where(me < n // 2, 1 - way, way)
        sub = lax.rem(i // 2, subs)
        step = i // (2 * subs)
        chunk = jnp.where(rightward == 1, n - 1 - step, step)
        active = jnp.where(rightward == 1, chunk > me, chunk < me)
        return rightward, chunk, sub, active

    def weight_copies(chunk, sub):
        at = chunk * subs + sub
        rows = pl.ds(pl.multiple_of(at * sub_rows, sub_rows), sub_rows)
        return [
            pltpu.make_async_copy(src.at[rows, :], dst.at[rows, :], w_sem.at[j, at])
            for j, (src, dst) in enumerate(((wq_ref, wq), (wk_ref, wk), (wv_ref, wv)))
        ]

    def remote(rightward, chunk, sub):
        slot = chunk * subs + sub
        to = jnp.where(rightward == 1, jnp.minimum(me + 1, n - 1), jnp.maximum(me - 1, 0))
        return [
            pltpu.make_async_remote_copy(
                src_ref=s.at[slot],
                dst_ref=r.at[rightward, slot],
                send_sem=ss.at[slot],
                recv_sem=rs.at[rightward, slot],
                device_id={"tp": to},
                device_id_type=MESH,
            )
            for s, r, ss, rs in (
                (send, recv, send_sem, recv_sem),
                (send_scale, recv_scale, send_scale_sem, recv_scale_sem),
            )
        ]

    def own_term(chunk, sub):
        for copy in weight_copies(chunk, sub):
            copy.wait()
        at = chunk * subs + sub
        rows = pl.ds(pl.multiple_of(at * sub_rows, sub_rows), sub_rows)
        half = wk.shape[1]
        contract = ((1,), (1,))
        total = dot(wq[rows, :], dq_ref[...], contract)
        total = total + dot(wk[rows, :], dkv_ref[:, :half], contract)
        acc[...] = total + dot(wv[rows, :], dkv_ref[:, half:], contract)

    def add_received(rightward, chunk, sub):
        for copy in remote(rightward, chunk, sub):
            copy.wait_recv()
        slot = chunk * subs + sub
        scale = recv_scale[rightward, slot, 0:1, :]
        acc[...] += recv[rightward, slot].astype(jnp.int32).astype(jnp.float32) * scale

    @pl.loop(0, steps)
    def _(i):
        _, chunk, sub, active = plan(i)

        @pl.when(active)
        def _():
            for copy in weight_copies(chunk, sub):
                copy.start()

    @pl.loop(0, subs)
    def _(sub):
        for copy in weight_copies(me, sub):
            copy.start()

    barrier = pltpu.get_barrier_semaphore()

    @pl.when(me > 0)
    def _():
        pl.semaphore_signal(barrier, inc=1, device_id={"tp": jnp.maximum(me - 1, 0)}, device_id_type=MESH)

    @pl.when(me < n - 1)
    def _():
        pl.semaphore_signal(barrier, inc=1, device_id={"tp": jnp.minimum(me + 1, n - 1)}, device_id_type=MESH)

    peers = jnp.where(me > 0, 1, 0) + jnp.where(me < n - 1, 1, 0)
    pl.semaphore_wait(barrier, peers)

    @pl.loop(0, steps)
    def _(i):
        rightward, chunk, sub, active = plan(i)

        @pl.when(active)
        def _():
            own_term(chunk, sub)

            @pl.when(jnp.where(rightward == 1, me > 0, me < n - 1))
            def _():
                add_received(rightward, chunk, sub)

            slot = chunk * subs + sub
            largest = jnp.maximum(jnp.max(jnp.abs(acc[...]), axis=0, keepdims=True), 1e-30)
            send_scale[slot] = jnp.broadcast_to(largest * (1.0 / 32767.0), send_scale.shape[1:])
            coded = jnp.round(acc[...] * (32767.0 / largest))
            send[slot] = coded.astype(jnp.int32).astype(jnp.int16)
            for copy in remote(rightward, chunk, sub):
                copy.start()

    @pl.loop(0, subs)
    def _(sub):
        own_term(me, sub)

        @pl.when(me > 0)
        def _():
            add_received(1, me, sub)

        @pl.when(me < n - 1)
        def _():
            add_received(0, me, sub)

        rows = pl.ds(pl.multiple_of(sub * sub_rows, sub_rows), sub_rows)
        out_ref[rows, :] = acc[...].astype(jnp.bfloat16)

    @pl.loop(0, steps)
    def _(i):
        rightward, chunk, sub, active = plan(i)

        @pl.when(active)
        def _():
            for copy in remote(rightward, chunk, sub):
                copy.wait_send()


def project(n, dq, dkv, w_query, key_weight, value_weight):
    tokens = dq.shape[0]
    width = w_query.shape[0]
    chunk_rows = width // n
    sub_rows = 320 if chunk_rows % 320 == 0 else chunk_rows
    slots = width // sub_rows
    vm = pl.BlockSpec(memory_space=pltpu.VMEM)
    hbm = pl.BlockSpec(memory_space=pl.ANY)
    dma = pltpu.SemaphoreType.DMA
    return pl.pallas_call(
        functools.partial(project_kernel, n),
        out_shape=jax.ShapeDtypeStruct((chunk_rows, tokens), jnp.bfloat16),
        in_specs=[vm, vm, hbm, hbm, hbm],
        out_specs=vm,
        scratch_shapes=[
            pltpu.VMEM(w_query.shape, jnp.bfloat16),
            pltpu.VMEM(key_weight.shape, jnp.bfloat16),
            pltpu.VMEM(value_weight.shape, jnp.bfloat16),
            pltpu.VMEM((sub_rows, tokens), jnp.float32),
            pltpu.VMEM((slots, sub_rows, tokens), jnp.int16),
            pltpu.VMEM((slots, 8, tokens), jnp.float32),
            pltpu.VMEM((2, slots, sub_rows, tokens), jnp.int16),
            pltpu.VMEM((2, slots, 8, tokens), jnp.float32),
            dma((3, slots)),
            dma((slots,)),
            dma((2, slots)),
            dma((slots,)),
            dma((2, slots)),
        ],
        compiler_params=pltpu.CompilerParams(
            collective_id=2, has_side_effects=True, vmem_limit_bytes=VMEM_BYTES
        ),
        name="project",
    )(dq, dkv, w_query, key_weight, value_weight)


def local(
    n_ctx,
    n_tp,
    query,
    key_projected,
    value,
    attention_output,
    output_gradient,
    lse,
    block_mask,
    positions,
    segments,
    w_query,
    key_weight,
    value_weight,
):
    tok_rows = query.shape[0]
    kv_local = key_projected.shape[1] // HEAD_SIZE
    heads_local = kv_local * GROUP
    kv_cols = kv_local * HEAD_SIZE
    q_start = lax.axis_index("ctx") * tok_rows
    cosine, sine = rope_tables(positions, HEAD_SIZE)
    key_three = key_projected.astype(jnp.float32).reshape(tok_rows, kv_local, HEAD_SIZE)
    key_rotated = (
        (key_three * cosine[:, None, :] + swap_halves(key_three) * sine[:, None, :])
        .astype(jnp.bfloat16)
        .reshape(tok_rows, kv_cols)
    )
    delta = jnp.sum(
        (output_gradient.astype(jnp.float32) * attention_output.astype(jnp.float32)).reshape(
            tok_rows, heads_local, HEAD_SIZE
        ),
        -1,
    ).T
    kv_whole = lax.all_gather(
        jnp.concatenate([key_rotated, value], 1), "ctx", axis=0, tiled=True
    )
    seg_row = lax.dynamic_slice_in_dim(segments, q_start, tok_rows).reshape(1, tok_rows)
    first_tile = (q_start // TILE).astype(jnp.int32).reshape(1)
    query_grad, terms = attention(
        first_tile, block_mask, query, output_gradient, lse, delta, cosine, sine, kv_whole, seg_row
    )
    summed = lax.psum_scatter(terms, "ctx", scatter_dimension=0, tiled=True)
    key_three = (summed[:, :kv_cols] * SCALE).reshape(tok_rows, kv_local, HEAD_SIZE)
    key_gradient = (key_three * cosine[:, None, :] - swap_halves(key_three) * sine[:, None, :]).reshape(
        tok_rows, kv_cols
    )
    dkv = jnp.concatenate([key_gradient, summed[:, kv_cols:]], 1).astype(jnp.bfloat16)
    return project(n_tp, query_grad, dkv, w_query, key_weight, value_weight)


def solution(mesh):
    in_specs = (
        P("ctx", "tp"),
        P("ctx", "tp"),
        P("ctx", "tp"),
        P("ctx", "tp"),
        P("ctx", "tp"),
        P("tp", "ctx"),
        P(),
        P("ctx"),
        P(),
        P(None, "tp"),
        P(None, "tp"),
        P(None, "tp"),
    )
    out_specs = P("tp", "ctx")
    body = functools.partial(local, mesh.shape["ctx"], mesh.shape["tp"])
    return jax.shard_map(body, mesh=mesh, in_specs=in_specs, out_specs=out_specs, check_vma=False)
```

time: 299 us -> 173 us (0.58)
  waiting for transfers between devices: 162 us -> 86.8 us
  Pallas kernels: 0 us -> 60.1 us
  local copies, waits for them, and re-layouts: 52.9 us -> 6.31 us
  matrix products: 44.3 us -> 0 us
  other arithmetic: 19.8 us -> 5.53 us
  loops' own time: 3 us -> 0 us
    reduce_scatter x1 -> x0, waiting for transfers between devices: 94 us -> none  [local(): lax.psum_scatter(result, 'tp', scatter_dimension=0, tiled=True)]
    pallas_call x0 -> x2, Pallas kernels: none -> 60.1 us  [the longest x1 51.6 us: project(): pl.pallas_call(functools.partial(project_kernel, n), out_shape=jax.ShapeD...]
    dot_general x23 -> x0, matrix products: 44.3 us -> none  [the longest x1 16.1 us: local(): lax.dot_general(w_query, query_grad, contract, preferred_element_type=jnp...]
    reduce_scatter x1, waiting for transfers between devices: 31 us -> 60.6 us  [local(): summed = lax.psum_scatter(terms, 'ctx', scatter_dimension=0, tiled=True)]
    dynamic_update_slice x8 -> x0, local copies, waits for them, and re-layouts: 19.4 us -> none  [local(): lax.scan(all_terms, query_empty, jnp.arange(key_total // key_step))]
    all_gather x2 -> x1, waiting for transfers between devices: 36.8 us -> 26.1 us  [local(): lax.all_gather(jnp.concatenate([key_rotated, value], 1), 'ctx', axis=0, t...]
    dynamic_slice x13 -> x1, local copies, waits for them, and re-layouts: 10.7 us -> 0.77 us  [local(): lax.dynamic_slice_in_dim(segments, q_start, tok_rows).reshape(1, tok_rows)]
    while x40 -> x0, local copies, waits for them, and re-layouts: 6.39 us -> none
  transfers between devices with their start and end apart: 4 -> 2, of which waited for: 4 -> 2; matrix products, arithmetic and copies ran while one was open for 11% -> 2% of each run, Pallas kernels for 0% -> 0%
where the time goes in v1:
time: 173 us; the launch traced here: 172 us
  waiting for transfers between devices  86.8 us (50%)
  Pallas kernels  60.1 us (35%)
  between operations  13.6 us (8%)
  local copies, waits for them, and re-layouts  6.31 us (4%)
  other arithmetic  5.53 us (3%)
    reduce_scatter x1, waiting for transfers between devices, local(): summed = lax.psum_scatter(terms, 'ctx', scatter_dimension=0, tiled=True)  60.6 us
    pallas_call x1, Pallas kernels, project(): pl.pallas_call(functools.partial(project_kernel, n), out_shape=jax.ShapeD...  51.6 us
    all_gather x1, waiting for transfers between devices, local(): lax.all_gather(jnp.concatenate([key_rotated, value], 1), 'ctx', axis=0, t...  26.1 us
    pallas_call x1, Pallas kernels, attention(): pl.pallas_call(attention_kernel, out_shape=(jax.ShapeDtypeStruct(query.sh...  8.47 us
  transfers between devices with their start and end apart: 2, of which 2 were waited for; matrix products, arithmetic and copies ran while one was open for 2% of the time, Pallas kernels for 0%

profile of v1, /device:TPU:12, one launch (start us, length us, event | category | flops | bytes accessed | tf_op | source)
XLA Modules:
  0.0 172.3 jit_solution(18410366059395619332)
XLA Ops:
  6.5 0.0 copy-start.6
  6.5 0.0 all-gather.2.cloned.1.call-start
  6.5 0.7 convert_element_type.26
  7.3 1.0 reshape.37
  8.3 0.0 copy-start.7
  8.3 0.3 fusion.4
  8.7 0.0 copy-start.5
  8.7 0.5 fusion.2
  9.2 0.1 pad_maximum_fusion.2
  9.3 0.0 copy-start.1
  9.4 0.0 copy-start.3
  9.4 0.0 copy-start
  9.4 0.4 maximum_multiply_fusion
  9.7 0.3 copy-done.1
  10.0 0.1 copy-done.3
  10.0 0.1 mul.82
  10.1 0.0 copy-done.6
  10.2 0.0 copy-done.7
  10.2 0.7 pad_maximum_fusion
  10.9 0.0 all-gather.2.cloned.1.call-update
  11.0 0.0 reduce-scatter.2.cloned.1.call-start
  11.0 0.8 dynamic_slice.3
  11.8 0.0 copy-start.8
  11.8 0.8 copy.15.segk_ref
  12.6 0.0 copy-done.5
  12.6 0.2 copy.14
  12.8 0.0 copy-done
  12.8 0.2 copy.13
  13.1 0.1 convert_multiply_fusion
  13.3 0.0 copy-done.8
  13.3 0.7 reduce_sum.9
  14.0 26.1 %all-gather.2.cloned.1.call-done.kv_ref = bf16[2048,512]{1,0:T(8,128)(2,1)} async-done(((bf16[256,512]{1,0:T(8,128)(2,1)}), bf16[2048,512]{1,0:T(8,128)(2,1)}) %all-gather.2.cloned.1.call-update) | async-done | bytes 2097168 | tf_op jit(solution)/shard_map/all_gather | solution.py:355
  40.1 8.5 %attention.1 = (bf16[256,1280]{1,0:T(8,128)(2,1)}, f32[2048,512]{1,0:T(8,128)}) custom-call(s32[1]{0:T(128)} %bitcast.start_ref, s32[16,16]{1,0:T(8,128)} %mask_ref.1, bf16[256,1280]{1,0:T(8,128)(2,1)} %q_ref.1, bf16[256,1280]{1,0:T(8,128)(2,1)} %do_ref.1, f32[10,256]{1,0:T(8,128)} %lse_ref.1, f32[10,256]{1,0:T(8,128)} %bitcast.28, f32[256,128]{1,0:T(8,128)} %copy-done.3, ...), custom_call_target="tpu_custom_call" | custom-call | tf_op jit(solution)/shard_map/attention/pallas_call | solution.py:127
  48.5 0.0 reduce-scatter.2.cloned.1.call-update
  48.5 0.0 copy-start.2
  48.6 60.6 %reduce-scatter.2.cloned.1.call-done = f32[256,512]{1,0:T(8,128)} async-done(((f32[2048,512]{1,0:T(8,128)}), f32[256,512]{1,0:T(8,128)}) %reduce-scatter.2.cloned.1.call-update) | async-done | bytes 524304 | tf_op jit(solution)/shard_map/reduce_scatter | solution.py:363
  109.2 0.0 copy-start.4
  109.2 1.0 slice_multiply_fusion
  110.2 0.1 reshape.39
  110.4 0.3 fusion.3
  110.7 0.0 copy-done.2
  110.7 0.4 maximum_multiply_fusion.1
  111.1 0.0 copy-done.4
  111.1 0.1 fusion
  111.2 0.7 pad_maximum_fusion.1.dkv_ref
  111.9 51.6 %project.1 = bf16[1280,256]{1,0:T(8,128)(2,1)} custom-call(bf16[256,1280]{1,0:T(8,128)(2,1)} %get-tuple-element.7.dq_ref, bf16[256,512]{1,0:T(8,128)(2,1)} %pad_maximum_fusion.1.dkv_ref, bf16[5120,1280]{1,0:T(8,128)(2,1)} %wq_ref.1, bf16[5120,256]{1,0:T(8,128)(2,1)} %wk_ref.1, bf16[5120,256]{1,0:T(8,128)(2,1)} %wv_ref.1), custom_call_target="tpu_custom_call" | custom-call | tf_op jit(solution)/shard_map/project/pallas_call | solution.py:294
  163.5 2.0 %copy.24 = bf16[1280,256]{1,0:T(8,128)(2,1)} copy(bf16[1280,256]{1,0:T(8,128)(2,1)} %project.1) | data formatting | bytes 1310720
  (3 shorter events, 0.1 us)
Async XLA Ops:
  6.5 3.6 %copy-start.6 = (bf16[256,256]{1,0:T(8,128)(2,1)S(1)}, bf16[256,256]{1,0:T(8,128)(2,1)}, u32[]{:S(2)}) copy-start(bf16[256,256]{1,0:T(8,128)(2,1)} %param.13) | copy-start | bytes 393220
  6.5 33.5 %all-gather.2.cloned.1.call-start = ((), (), s32[]{:S(2)}) async-start(), calls=%async_computation.1 | async-start | bytes 2359296 | tf_op jit(solution)/shard_map/all_gather | solution.py:355
  8.3 1.9 %copy-start.7 = (bf16[256,256]{1,0:T(8,128)(2,1)S(1)}, bf16[256,256]{1,0:T(8,128)(2,1)}, u32[]{:S(2)}) copy-start(bf16[256,256]{1,0:T(8,128)(2,1)} %param.14) | copy-start | bytes 393220
  8.7 3.9 %copy-start.5 = (bf16[256,1280]{1,0:T(8,128)(2,1)S(1)}, bf16[256,1280]{1,0:T(8,128)(2,1)}, u32[]{:S(2)}) copy-start(bf16[256,1280]{1,0:T(8,128)(2,1)} %param.15) | copy-start | bytes 1966084
  9.3 0.6 copy-start.1
  9.4 0.7 copy-start.3
  9.4 3.5 %copy-start = (bf16[256,1280]{1,0:T(8,128)(2,1)S(1)}, bf16[256,1280]{1,0:T(8,128)(2,1)}, u32[]{:S(2)}) copy-start(bf16[256,1280]{1,0:T(8,128)(2,1)} %do_ref.1) | copy-start | bytes 1966084
  11.0 98.2 %reduce-scatter.2.cloned.1.call-start = ((), (), s32[]{:S(2)}) async-start(), calls=%async_computation.2 | async-start | bytes 4718592 | tf_op jit(solution)/shard_map/reduce_scatter | solution.py:363
  11.8 1.5 copy-start.8
  48.5 62.2 %copy-start.2 = (f32[256,128]{1,0:T(8,128)S(1)}, f32[256,128]{1,0:T(8,128)}, u32[]{:S(2)}) copy-start(f32[256,128]{1,0:T(8,128)} %copy-done.1) | copy-start | bytes 393220
  109.2 1.9 %copy-start.4 = (f32[256,512]{1,0:T(8,128)S(1)}, f32[256,512]{1,0:T(8,128)}, u32[]{:S(2)}) copy-start(f32[256,512]{1,0:T(8,128)} %reduce-scatter.2.cloned.1.call-done) | copy-start | bytes 1572868
Sparse Core Ops, SparseCore 0:
  11.1 28.9 all-gather.1
  48.7 60.4 reduce-scatter.1

commit v2 on v1

--- a/solution.py
+++ b/solution.py
@@ -15,6 +15,7 @@
 SCALE = HEAD_SIZE ** (-0.5)
 MESH = pl.DeviceIdType.MESH
 VMEM_BYTES = 56 * 1024 * 1024
+ATTENTION_BYTES = 24 * 1024 * 1024
 
 rope_base = 1000000.0
 
@@ -32,44 +33,152 @@
     )
 
 
-def swap_halves(x):
-    half = HEAD_SIZE // 2
-    return jnp.concatenate([x[..., half:], x[..., :half]], -1)
-
-
 def dot(a, b, dims=((1,), (0,))):
     return lax.dot_general(a, b, (dims, ((), ())), preferred_element_type=jnp.float32)
 
 
+def gather_kernel(
+    n, kp_ref, v_ref, q_ref, do_ref, ao_ref, cos_ref, sin_ref,
+    kv_ref, qs_ref, dos_ref, qt_ref, dot_ref, delta_ref,
+    send_sem, recv_sem, pass_sem, pass_recv_sem,
+):
+    me = lax.axis_index("ctx")
+    chip, core = me // 2, lax.rem(me, 2)
+    sibling = 2 * chip + 1 - core
+    chips = n // 2
+    tokens, kv_cols = kp_ref.shape
+    heads = q_ref.shape[1] // HEAD_SIZE
+    q_tiles = tokens // TILE
+
+    barrier = pltpu.get_barrier_semaphore()
+    for away in range(1, chips):
+        other = 2 * lax.rem(chip + away, chips) + core
+        pl.semaphore_signal(barrier, inc=1, device_id={"ctx": other}, device_id_type=MESH)
+    pl.semaphore_signal(barrier, inc=1, device_id={"ctx": sibling}, device_id_type=MESH)
+
+    for c in range(kv_cols // HEAD_SIZE):
+        cols = slice(c * HEAD_SIZE, (c + 1) * HEAD_SIZE)
+        x = kp_ref[:, cols].astype(jnp.float32)
+        x = x * cos_ref[...] + pltpu.roll(x, HEAD_SIZE // 2, 1) * sin_ref[...]
+        kv_ref[me, :, cols] = x.astype(jnp.bfloat16)
+    kv_ref[me, :, kv_cols:] = v_ref[...]
+
+    def direct(source, target):
+        slot = 2 * source + core
+        return pltpu.make_async_remote_copy(
+            src_ref=kv_ref.at[slot],
+            dst_ref=kv_ref.at[slot],
+            send_sem=send_sem.at[target],
+            recv_sem=recv_sem.at[source],
+            device_id={"ctx": 2 * target + core},
+            device_id_type=MESH,
+        )
+
+    def handed(source, from_core):
+        slot = 2 * source + from_core
+        return pltpu.make_async_remote_copy(
+            src_ref=kv_ref.at[slot],
+            dst_ref=kv_ref.at[slot],
+            send_sem=pass_sem.at[source],
+            recv_sem=pass_recv_sem.at[source],
+            device_id={"ctx": sibling},
+            device_id_type=MESH,
+        )
+
+    pl.semaphore_wait(barrier, chips)
+    for away in range(chips - 1, 0, -1):
+
+        @pl.when(chip + away < chips)
+        def _():
+            direct(chip, jnp.minimum(chip + away, chips - 1)).start()
+
+    handed(chip, core).start()
+
+    @pl.loop(0, q_tiles * heads)
+    def _(i):
+        t, h = i // heads, lax.rem(i, heads)
+        c, g = h // GROUP, lax.rem(h, GROUP)
+        rows = pl.ds(pl.multiple_of(t * TILE, TILE), TILE)
+        cols = pl.ds(pl.multiple_of(h * HEAD_SIZE, HEAD_SIZE), HEAD_SIZE)
+        part = pl.ds(pl.multiple_of(g * TILE, TILE), TILE)
+        x = q_ref[rows, cols].astype(jnp.float32)
+        x = x * cos_ref[rows, :] + pltpu.roll(x, HEAD_SIZE // 2, 1) * sin_ref[rows, :]
+        xb = x.astype(jnp.bfloat16)
+        qs_ref[t, c, part, :] = xb
+        qt_ref[t, c, :, part] = xb.astype(jnp.float32).T.astype(jnp.bfloat16)
+        y = do_ref[rows, cols]
+        dos_ref[t, c, part, :] = y
+        y_turned = y.astype(jnp.float32).T
+        dot_ref[t, c, :, part] = y_turned.astype(jnp.bfloat16)
+        o_turned = ao_ref[rows, cols].astype(jnp.float32).T
+        delta_ref[t, c, :, part] = jnp.sum(y_turned * o_turned, axis=0, keepdims=True)
+
+    for away in range(1, chips):
+
+        @pl.when(chip - away >= 0)
+        def _():
+            source = jnp.maximum(chip - away, 0)
+            direct(source, chip).wait_recv()
+            handed(source, core).start()
+
+    for away in range(chips):
+
+        @pl.when(chip - away >= 0)
+        def _():
+            source = jnp.maximum(chip - away, 0)
+            handed(source, 1 - core).wait_recv()
+            handed(source, core).wait_send()
+
+    for away in range(1, chips):
+
+        @pl.when(chip + away < chips)
+        def _():
+            direct(chip, jnp.minimum(chip + away, chips - 1)).wait_send()
+
+
+def gather(n, key_projected, value, query, grad, attention_output, cosine, sine):
+    tokens, kv_cols = key_projected.shape
+    kv_local = kv_cols // HEAD_SIZE
+    q_tiles = tokens // TILE
+    wide = GROUP * TILE
+    vm = pl.BlockSpec(memory_space=pltpu.VMEM)
+    dma = pltpu.SemaphoreType.DMA
+    stacked = jax.ShapeDtypeStruct((q_tiles, kv_local, wide, HEAD_SIZE), jnp.bfloat16)
+    turned = jax.ShapeDtypeStruct((q_tiles, kv_local, HEAD_SIZE, wide), jnp.bfloat16)
+    return pl.pallas_call(
+        functools.partial(gather_kernel, n),
+        out_shape=(
+            jax.ShapeDtypeStruct((n, tokens, 2 * kv_cols), jnp.bfloat16),
+            stacked,
+            stacked,
+            turned,
+            turned,
+            jax.ShapeDtypeStruct((q_tiles, kv_local, 1, wide), jnp.float32),
+        ),
+        in_specs=[vm] * 7,
+        out_specs=(vm,) * 6,
+        scratch_shapes=[dma((n // 2,))] * 4,
+        compiler_params=pltpu.CompilerParams(
+            collective_id=1, has_side_effects=True, vmem_limit_bytes=ATTENTION_BYTES
+        ),
+        name="gather",
+    )(key_projected, value, query, grad, attention_output, cosine, sine)
+
+
 def attention_kernel(
-    start_ref, mask_ref, q_ref, do_ref, lse_ref, delta_ref, cos_ref, sin_ref, kv_ref, segq_ref, segk_ref,
-    dq_ref, dkv_ref, qs, dos, qt_s, dot_s, lse_s, delta_s, dqt,
+    start_ref, mask_ref, qs, dos, qt_s, dot_s, lse_ref, delta_s, cos_ref, sin_ref, kv_ref, segq_ref, segk_ref,
+    dq_ref, dkv_ref, lse_s, dqt,
 ):
-    tokens = q_ref.shape[0]
+    tokens = dq_ref.shape[0]
     kv_local = kv_ref.shape[1] // (2 * HEAD_SIZE)
     q_tiles = tokens // TILE
-    wide = GROUP * TILE
     first_tile = start_ref[0]
     dkv_ref[...] = jnp.zeros_like(dkv_ref)
     dqt[...] = jnp.zeros_like(dqt)
     for t in range(q_tiles):
-        rows = slice(t * TILE, (t + 1) * TILE)
-        cosine = cos_ref[rows, :]
-        sine = sin_ref[rows, :]
         for h in range(kv_local * GROUP):
             c, g = h // GROUP, h % GROUP
-            part = slice(g * TILE, (g + 1) * TILE)
-            cols = slice(h * HEAD_SIZE, (h + 1) * HEAD_SIZE)
-            x = q_ref[rows, cols].astype(jnp.float32)
-            x = x * cosine + pltpu.roll(x, HEAD_SIZE // 2, 1) * sine
-            xb = x.astype(jnp.bfloat16)
-            qs[t, c, part, :] = xb
-            qt_s[t, c, :, part] = xb.astype(jnp.float32).T.astype(jnp.bfloat16)
-            y = do_ref[rows, cols]
-            dos[t, c, part, :] = y
-            dot_s[t, c, :, part] = y.astype(jnp.float32).T.astype(jnp.bfloat16)
-            lse_s[t, c, :, part] = lse_ref[h : h + 1, rows]
-            delta_s[t, c, :, part] = delta_ref[h : h + 1, rows]
+            lse_s[t, c, :, g * TILE : (g + 1) * TILE] = lse_ref[h : h + 1, t * TILE : (t + 1) * TILE]
 
     def pair(t, k_tile, allowed):
         k_rows = pl.ds(pl.multiple_of(k_tile * TILE, TILE), TILE)
@@ -117,41 +226,47 @@
             dq_ref[rows, h * HEAD_SIZE : (h + 1) * HEAD_SIZE] = x.astype(jnp.bfloat16)
 
 
-def attention(first_tile, block_mask, query, grad, lse, delta, cosine, sine, kv_whole, seg_row):
-    tokens = query.shape[0]
-    kv_local = kv_whole.shape[1] // (2 * HEAD_SIZE)
-    q_tiles = tokens // TILE
-    wide = GROUP * TILE
+def attention(first_tile, block_mask, prepared, lse, cosine, sine, kv_whole, seg_row):
+    qs, dos, turned_q, turned_do, delta = prepared
+    q_tiles, kv_local, wide, _ = qs.shape
+    tokens = q_tiles * TILE
     vm = pl.BlockSpec(memory_space=pltpu.VMEM)
     sm = pl.BlockSpec(memory_space=pltpu.SMEM)
     return pl.pallas_call(
         attention_kernel,
         out_shape=(
-            jax.ShapeDtypeStruct(query.shape, jnp.bfloat16),
+            jax.ShapeDtypeStruct((tokens, kv_local * GROUP * HEAD_SIZE), jnp.bfloat16),
             jax.ShapeDtypeStruct(kv_whole.shape, jnp.float32),
         ),
-        in_specs=[sm, sm] + [vm] * 9,
+        in_specs=[sm, sm] + [vm] * 11,
         out_specs=(vm, vm),
         scratch_shapes=[
-            pltpu.VMEM((q_tiles, kv_local, wide, HEAD_SIZE), jnp.bfloat16),
-            pltpu.VMEM((q_tiles, kv_local, wide, HEAD_SIZE), jnp.bfloat16),
-            pltpu.VMEM((q_tiles, kv_local, HEAD_SIZE, wide), jnp.bfloat16),
-            pltpu.VMEM((q_tiles, kv_local, HEAD_SIZE, wide), jnp.bfloat16),
-            pltpu.VMEM((q_tiles, kv_local, 1, wide), jnp.float32),
             pltpu.VMEM((q_tiles, kv_local, 1, wide), jnp.float32),
             pltpu.VMEM((q_tiles, kv_local, HEAD_SIZE, wide), jnp.float32),
         ],
-        compiler_params=pltpu.CompilerParams(vmem_limit_bytes=VMEM_BYTES),
+        compiler_params=pltpu.CompilerParams(vmem_limit_bytes=ATTENTION_BYTES),
         name="attention",
-    )(first_tile, block_mask, query, grad, lse, delta, cosine, sine, kv_whole, seg_row, seg_row.reshape(tokens, 1))
+    )(
+        first_tile, block_mask, qs, dos, turned_q, turned_do, lse, delta, cosine, sine, kv_whole,
+        seg_row, seg_row.reshape(tokens, 1),
+    )
 
 
 def project_kernel(
-    n, dq_ref, dkv_ref, wq_ref, wk_ref, wv_ref, out_ref,
+    n_ctx, n, dq_ref, terms_ref, cos_ref, sin_ref, wq_ref, wk_ref, wv_ref, out_ref,
     wq, wk, wv, acc, send, send_scale, recv, recv_scale,
+    dkv_ref, total, near, part, part_scale, far, far_scale,
     w_sem, send_sem, recv_sem, send_scale_sem, recv_scale_sem,
+    near_send_sem, near_sem, part_sem, far_sem, part_scale_sem, far_scale_sem,
 ):
     me = lax.axis_index("tp")
+    chips = n_ctx // 2
+    place = lax.axis_index("ctx")
+    chip, core = place // 2, lax.rem(place, 2)
+    sibling = 2 * chip + 1 - core
+    tokens, kv_width = dkv_ref.shape
+    kv_half = kv_width // 2
+    group = tokens // 8
     chunk_rows = out_ref.shape[0]
     sub_rows = acc.shape[0]
     subs = chunk_rows // sub_rows
@@ -234,8 +349,86 @@
     def _():
         pl.semaphore_signal(barrier, inc=1, device_id={"tp": jnp.minimum(me + 1, n - 1)}, device_id_type=MESH)
 
-    peers = jnp.where(me > 0, 1, 0) + jnp.where(me < n - 1, 1, 0)
+    for away in range(1, chips):
+        other = 2 * lax.rem(chip + away, chips) + core
+        pl.semaphore_signal(barrier, inc=1, device_id={"ctx": other}, device_id_type=MESH)
+    pl.semaphore_signal(barrier, inc=1, device_id={"ctx": sibling}, device_id_type=MESH)
+    peers = jnp.where(me > 0, 1, 0) + jnp.where(me < n - 1, 1, 0) + chips
     pl.semaphore_wait(barrier, peers)
+
+    def token_rows(block):
+        return pl.ds(pl.multiple_of(block * tokens, tokens), tokens)
+
+    def to_sibling(j):
+        return pltpu.make_async_remote_copy(
+            src_ref=terms_ref.at[token_rows(2 * j + 1 - core), :],
+            dst_ref=near.at[j],
+            send_sem=near_send_sem.at[j],
+            recv_sem=near_sem.at[j],
+            device_id={"ctx": sibling},
+            device_id_type=MESH,
+        )
+
+    def to_owner(source, j):
+        return [
+            pltpu.make_async_remote_copy(
+                src_ref=p.at[j],
+                dst_ref=f.at[source],
+                send_sem=ps.at[j],
+                recv_sem=fs.at[source],
+                device_id={"ctx": 2 * j + core},
+                device_id_type=MESH,
+            )
+            for p, f, ps, fs in (
+                (part, far, part_sem, far_sem),
+                (part_scale, far_scale, part_scale_sem, far_scale_sem),
+            )
+        ]
+
+    @pl.loop(0, chip + 1)
+    def _(j):
+        to_sibling(j).start()
+
+    @pl.loop(0, chip)
+    def _(j):
+        to_sibling(j).wait_recv()
+        for r in range(8):
+            rows = slice(r * group, (r + 1) * group)
+            at = pl.ds(pl.multiple_of((2 * j + core) * tokens + r * group, group), group)
+            x = terms_ref[at, :] + near[j, rows, :]
+            largest = jnp.maximum(jnp.max(jnp.abs(x), axis=0, keepdims=True), 1e-30)
+            part_scale[j, r : r + 1, :] = largest * (1.0 / 32767.0)
+            part[j, rows, :] = jnp.round(x * (32767.0 / largest)).astype(jnp.int32).astype(jnp.int16)
+        for copy in to_owner(chip, j):
+            copy.start()
+
+    to_sibling(chip).wait_recv()
+    total[...] = terms_ref[token_rows(place), :] + near[chip]
+
+    @pl.loop(chip + 1, chips)
+    def _(j):
+        for copy in to_owner(j, chip):
+            copy.wait_recv()
+        for r in range(8):
+            rows = slice(r * group, (r + 1) * group)
+            x = far[j, rows, :].astype(jnp.int32).astype(jnp.float32)
+            total[rows, :] += x * far_scale[j, r : r + 1, :]
+
+    for c in range(kv_half // HEAD_SIZE):
+        cols = slice(c * HEAD_SIZE, (c + 1) * HEAD_SIZE)
+        x = total[:, cols] * SCALE
+        x = x * cos_ref[...] - pltpu.roll(x, HEAD_SIZE // 2, 1) * sin_ref[...]
+        dkv_ref[:, cols] = x.astype(jnp.bfloat16)
+    dkv_ref[:, kv_half:] = total[:, kv_half:].astype(jnp.bfloat16)
+
+    @pl.loop(0, chip + 1)
+    def _(j):
+        to_sibling(j).wait_send()
+
+    @pl.loop(0, chip)
+    def _(j):
+        for copy in to_owner(chip, j):
+            copy.wait_send()
 
     @pl.loop(0, steps)
     def _(i):
@@ -282,8 +475,10 @@
                 copy.wait_send()
 
 
-def project(n, dq, dkv, w_query, key_weight, value_weight):
+def project(n_ctx, n, dq, terms, cosine, sine, w_query, key_weight, value_weight):
     tokens = dq.shape[0]
+    kv_width = terms.shape[1]
+    chips = n_ctx // 2
     width = w_query.shape[0]
     chunk_rows = width // n
     sub_rows = 320 if chunk_rows % 320 == 0 else chunk_rows
@@ -292,9 +487,9 @@
     hbm = pl.BlockSpec(memory_space=pl.ANY)
     dma = pltpu.SemaphoreType.DMA
     return pl.pallas_call(
-        functools.partial(project_kernel, n),
+        functools.partial(project_kernel, n_ctx, n),
         out_shape=jax.ShapeDtypeStruct((chunk_rows, tokens), jnp.bfloat16),
-        in_specs=[vm, vm, hbm, hbm, hbm],
+        in_specs=[vm, vm, vm, vm, hbm, hbm, hbm],
         out_specs=vm,
         scratch_shapes=[
             pltpu.VMEM(w_query.shape, jnp.bfloat16),
@@ -305,17 +500,25 @@
             pltpu.VMEM((slots, 8, tokens), jnp.float32),
             pltpu.VMEM((2, slots, sub_rows, tokens), jnp.int16),
             pltpu.VMEM((2, slots, 8, tokens), jnp.float32),
+            pltpu.VMEM((tokens, kv_width), jnp.bfloat16),
+            pltpu.VMEM((tokens, kv_width), jnp.float32),
+            pltpu.VMEM((chips, tokens, kv_width), jnp.float32),
+            pltpu.VMEM((chips, tokens, kv_width), jnp.int16),
+            pltpu.VMEM((chips, 8, kv_width), jnp.float32),
+            pltpu.VMEM((chips, tokens, kv_width), jnp.int16),
+            pltpu.VMEM((chips, 8, kv_width), jnp.float32),
             dma((3, slots)),
             dma((slots,)),
             dma((2, slots)),
             dma((slots,)),
             dma((2, slots)),
-        ],
+        ]
+        + [dma((chips,))] * 6,
         compiler_params=pltpu.CompilerParams(
             collective_id=2, has_side_effects=True, vmem_limit_bytes=VMEM_BYTES
         ),
         name="project",
-    )(dq, dkv, w_query, key_weight, value_weight)
+    )(dq, terms, cosine, sine, w_query, key_weight, value_weight)
 
 
 def local(
@@ -335,38 +538,18 @@
     value_weight,
 ):
     tok_rows = query.shape[0]
-    kv_local = key_projected.shape[1] // HEAD_SIZE
-    heads_local = kv_local * GROUP
-    kv_cols = kv_local * HEAD_SIZE
     q_start = lax.axis_index("ctx") * tok_rows
     cosine, sine = rope_tables(positions, HEAD_SIZE)
-    key_three = key_projected.astype(jnp.float32).reshape(tok_rows, kv_local, HEAD_SIZE)
-    key_rotated = (
-        (key_three * cosine[:, None, :] + swap_halves(key_three) * sine[:, None, :])
-        .astype(jnp.bfloat16)
-        .reshape(tok_rows, kv_cols)
+    kv_blocks, *prepared = gather(
+        n_ctx, key_projected, value, query, output_gradient, attention_output, cosine, sine
     )
-    delta = jnp.sum(
-        (output_gradient.astype(jnp.float32) * attention_output.astype(jnp.float32)).reshape(
-            tok_rows, heads_local, HEAD_SIZE
-        ),
-        -1,
-    ).T
-    kv_whole = lax.all_gather(
-        jnp.concatenate([key_rotated, value], 1), "ctx", axis=0, tiled=True
-    )
+    kv_whole = kv_blocks.reshape(n_ctx * tok_rows, kv_blocks.shape[-1])
     seg_row = lax.dynamic_slice_in_dim(segments, q_start, tok_rows).reshape(1, tok_rows)
     first_tile = (q_start // TILE).astype(jnp.int32).reshape(1)
     query_grad, terms = attention(
-        first_tile, block_mask, query, output_gradient, lse, delta, cosine, sine, kv_whole, seg_row
+        first_tile, block_mask, prepared, lse, cosine, sine, kv_whole, seg_row
     )
-    summed = lax.psum_scatter(terms, "ctx", scatter_dimension=0, tiled=True)
-    key_three = (summed[:, :kv_cols] * SCALE).reshape(tok_rows, kv_local, HEAD_SIZE)
-    key_gradient = (key_three * cosine[:, None, :] - swap_halves(key_three) * sine[:, None, :]).reshape(
-        tok_rows, kv_cols
-    )
-    dkv = jnp.concatenate([key_gradient, summed[:, kv_cols:]], 1).astype(jnp.bfloat16)
-    return project(n_tp, query_grad, dkv, w_query, key_weight, value_weight)
+    return project(n_ctx, n_tp, query_grad, terms, cosine, sine, w_query, key_weight, value_weight)
 
 
 def solution(mesh):

time: 173 us -> 111 us (0.64)
  the two profiles are of different devices: /device:TPU:12 before, /device:TPU:18 now
where the time goes in v2:
time: 111 us
  Pallas kernels  98.5 us (89%)
  local copies, waits for them, and re-layouts  10.8 us (10%)
  other arithmetic  1.37 us (1%)
    pallas_call x1, Pallas kernels, project(): pl.pallas_call(functools.partial(project_kernel, n_ctx, n), out_shape=jax...  72.4 us
    pallas_call x1, Pallas kernels, gather(): pl.pallas_call(functools.partial(gather_kernel, n), out_shape=(jax.ShapeD...  16 us
    pallas_call x1, Pallas kernels, attention(): pl.pallas_call(attention_kernel, out_shape=(jax.ShapeDtypeStruct((tokens,...  10.1 us
    unnamed x23, local copies, waits for them, and re-layouts  9.91 us

profile of v2, /device:TPU:18, one launch (start us, length us, event | category | flops | bytes accessed | tf_op | source)
XLA Modules:
  0.0 110.8 jit_solution(12518977082083021961)
XLA Ops:
  0.0 0.0 copy-start.10
  0.0 0.0 copy-start.9
  0.0 0.8 dynamic_slice.3
  0.8 0.7 convert_element_type.10
  1.5 0.1 copy.13.segk_ref
  1.6 0.5 fusion
  2.2 0.1 pad_maximum_fusion
  2.3 0.0 copy-start.1
  2.3 0.0 copy-start.2
  2.3 0.0 copy-start.4
  2.3 1.2 %copy-done.4 = bf16[256,1280]{1,0:T(8,128)(2,1)S(1)} copy-done((bf16[256,1280]{1,0:T(8,128)(2,1)S(1)}, bf16[256,1280]{1,0:T(8,128)(2,1)}, u32[]{:S(2)}) %copy-start.4) | copy-done | bytes 655384
  3.5 0.0 copy-start.5
  3.5 1.1 copy-done.5
  4.6 0.0 copy-start.6
  4.6 1.1 copy-done.6
  5.7 0.0 copy-start.7
  5.7 0.9 copy-done.7
  6.6 0.0 copy-start.8
  6.6 0.9 copy-done.8
  7.5 16.0 %gather.1 = (bf16[8,256,512]{2,1,0:T(8,128)(2,1)S(1)}, bf16[2,2,640,128]{3,2,1,0:T(8,128)(2,1)S(1)}, bf16[2,2,640,128]{3,2,1,0:T(8,128)(2,1)S(1)}, bf16[2,2,128,...) custom-call(bf16[256,256]{1,0:T(8,128)(2,1)S(1)} %copy-done.7, ...), custom_call_target="tpu_custom_call" | custom-call | tf_op jit(solution)/shard_map/gather/pallas_call | solution.py:148
  23.5 0.0 copy-done.10
  23.5 0.0 copy-done.9
  23.5 10.1 %attention.1 = (bf16[256,1280]{1,0:T(8,128)(2,1)S(1)}, f32[2048,512]{1,0:T(8,128)S(1)}) custom-call(s32[1]{0:T(128)} %bitcast.start_ref, s32[16,16]{1,0:T(8,128)S(1)} %copy-done.10, bf16[2,2,640,128]{3,2,1,0:T(8,128)(2,1)S(1)} %get-tuple-element.13.qs, bf16[2,2,640,128]{3,2,1,0:T(8,128)(2,1)S(1)} %get-tuple-element.14.dos, ...), custom_call_target="tpu_custom_call" | custom-call | tf_op jit(solution)/shard_map/attention/pallas_call | solution.py:235
  33.6 0.0 copy-done.1
  33.6 0.0 copy-done.2
  33.6 0.0 copy-start
  33.6 1.9 %copy-done = f32[2048,512]{1,0:T(8,128)} copy-done((f32[2048,512]{1,0:T(8,128)}, f32[2048,512]{1,0:T(8,128)S(1)}, u32[]{:S(2)}) %copy-start) | copy-done | bytes 4194328
  35.6 0.0 copy-start.3
  35.6 0.8 copy-done.3
  36.4 72.4 %project.1 = bf16[1280,256]{1,0:T(8,128)(2,1)} custom-call(bf16[256,1280]{1,0:T(8,128)(2,1)} %copy-done.3, f32[2048,512]{1,0:T(8,128)} %copy-done, f32[256,128]{1,0:T(8,128)} %copy-done.1, f32[256,128]{1,0:T(8,128)} %copy-done.2, bf16[5120,1280]{1,0:T(8,128)(2,1)} %wq_ref.1, bf16[5120,256]{1,0:T(8,128)(2,1)} %wk_ref.1, bf16[5120,256]{1,0:T(8,128)(2,1)} %wv_ref.1), custom_call_target="tpu_custom_call" | custom-call | tf_op jit(solution)/shard_map/project/pallas_call | solution.py:489
  108.8 2.0 %copy.15 = bf16[1280,256]{1,0:T(8,128)(2,1)} copy(bf16[1280,256]{1,0:T(8,128)(2,1)} %project.1) | data formatting | bytes 1310720
  (1 shorter events, 0.0 us)
Async XLA Ops:
  0.0 23.5 %copy-start.10 = (s32[16,16]{1,0:T(8,128)S(1)}, s32[16,16]{1,0:T(8,128)}, u32[]{:S(2)}) copy-start(s32[16,16]{1,0:T(8,128)} %mask_ref.1) | copy-start | bytes 3076
  0.0 23.5 %copy-start.9 = (f32[10,256]{1,0:T(8,128)S(1)}, f32[10,256]{1,0:T(8,128)}, u32[]{:S(2)}) copy-start(f32[10,256]{1,0:T(8,128)} %lse_ref.1) | copy-start | bytes 30724
  2.3 31.3 %copy-start.1 = (f32[256,128]{1,0:T(8,128)}, f32[256,128]{1,0:T(8,128)S(1)}, u32[]{:S(2)}) copy-start(f32[256,128]{1,0:T(8,128)S(1)} %get-tuple-element.24.cos_ref) | copy-start | bytes 393220
  2.3 31.3 %copy-start.2 = (f32[256,128]{1,0:T(8,128)}, f32[256,128]{1,0:T(8,128)S(1)}, u32[]{:S(2)}) copy-start(f32[256,128]{1,0:T(8,128)S(1)} %get-tuple-element.25.sin_ref) | copy-start | bytes 393220
  2.3 1.2 %copy-start.4 = (bf16[256,1280]{1,0:T(8,128)(2,1)S(1)}, bf16[256,1280]{1,0:T(8,128)(2,1)}, u32[]{:S(2)}) copy-start(bf16[256,1280]{1,0:T(8,128)(2,1)} %q_ref.1) | copy-start | bytes 1966084
  3.5 1.1 copy-start.5
  4.6 1.1 copy-start.6
  5.7 0.9 copy-start.7
  6.6 0.9 copy-start.8
  33.6 1.9 %copy-start = (f32[2048,512]{1,0:T(8,128)}, f32[2048,512]{1,0:T(8,128)S(1)}, u32[]{:S(2)}) copy-start(f32[2048,512]{1,0:T(8,128)S(1)} %get-tuple-element.20.terms_ref) | copy-start | bytes 12582916
  35.6 0.8 copy-start.3

commit v3 on v2

--- a/solution.py
+++ b/solution.py
@@ -38,10 +38,16 @@
 
 
 def gather_kernel(
-    n, kp_ref, v_ref, q_ref, do_ref, ao_ref, cos_ref, sin_ref,
+    n, kp_ref, v_ref, q_hbm, do_hbm, ao_hbm, cos_ref, sin_ref,
     kv_ref, qs_ref, dos_ref, qt_ref, dot_ref, delta_ref,
-    send_sem, recv_sem, pass_sem, pass_recv_sem,
+    q_ref, do_ref, ao_ref, load_sem, send_sem, recv_sem, pass_sem, pass_recv_sem,
 ):
+    loads = [
+        pltpu.make_async_copy(src, dst, load_sem.at[j])
+        for j, (src, dst) in enumerate(((q_hbm, q_ref), (do_hbm, do_ref), (ao_hbm, ao_ref)))
+    ]
+    for copy in loads:
+        copy.start()
     me = lax.axis_index("ctx")
     chip, core = me // 2, lax.rem(me, 2)
     sibling = 2 * chip + 1 - core
@@ -93,6 +99,8 @@
             direct(chip, jnp.minimum(chip + away, chips - 1)).start()
 
     handed(chip, core).start()
+    for copy in loads:
+        copy.wait()
 
     @pl.loop(0, q_tiles * heads)
     def _(i):
@@ -142,6 +150,7 @@
     q_tiles = tokens // TILE
     wide = GROUP * TILE
     vm = pl.BlockSpec(memory_space=pltpu.VMEM)
+    hbm = pl.BlockSpec(memory_space=pl.ANY)
     dma = pltpu.SemaphoreType.DMA
     stacked = jax.ShapeDtypeStruct((q_tiles, kv_local, wide, HEAD_SIZE), jnp.bfloat16)
     turned = jax.ShapeDtypeStruct((q_tiles, kv_local, HEAD_SIZE, wide), jnp.bfloat16)
@@ -155,9 +164,9 @@
             turned,
             jax.ShapeDtypeStruct((q_tiles, kv_local, 1, wide), jnp.float32),
         ),
-        in_specs=[vm] * 7,
+        in_specs=[vm, vm, hbm, hbm, hbm, vm, vm],
         out_specs=(vm,) * 6,
-        scratch_shapes=[dma((n // 2,))] * 4,
+        scratch_shapes=[pltpu.VMEM(query.shape, jnp.bfloat16)] * 3 + [dma((3,))] + [dma((n // 2,))] * 4,
         compiler_params=pltpu.CompilerParams(
             collective_id=1, has_side_effects=True, vmem_limit_bytes=ATTENTION_BYTES
         ),
@@ -167,7 +176,7 @@
 
 def attention_kernel(
     start_ref, mask_ref, qs, dos, qt_s, dot_s, lse_ref, delta_s, cos_ref, sin_ref, kv_ref, segq_ref, segk_ref,
-    dq_ref, dkv_ref, lse_s, dqt,
+    dq_ref, dkv_ref, lse_s, dqt, needed_ref,
 ):
     tokens = dq_ref.shape[0]
     kv_local = kv_ref.shape[1] // (2 * HEAD_SIZE)
@@ -180,13 +189,13 @@
             c, g = h // GROUP, h % GROUP
             lse_s[t, c, :, g * TILE : (g + 1) * TILE] = lse_ref[h : h + 1, t * TILE : (t + 1) * TILE]
 
-    def pair(t, k_tile, allowed):
-        k_rows = pl.ds(pl.multiple_of(k_tile * TILE, TILE), TILE)
+    def terms(t, k_tiles, allowed):
+        spans = [pl.ds(pl.multiple_of(k * TILE, TILE), TILE) for k in k_tiles]
         for c in range(kv_local):
             key_cols = slice(c * HEAD_SIZE, (c + 1) * HEAD_SIZE)
             val_cols = slice((kv_local + c) * HEAD_SIZE, (kv_local + c + 1) * HEAD_SIZE)
-            k = kv_ref[k_rows, key_cols]
-            v = kv_ref[k_rows, val_cols]
+            k = jnp.concatenate([kv_ref[span, key_cols] for span in spans], 0)
+            v = jnp.concatenate([kv_ref[span, val_cols] for span in spans], 0)
             scores = dot(k, qt_s[t, c]) * SCALE
             probs = jnp.exp(scores - lse_s[t, c])
             if allowed is not None:
@@ -194,27 +203,42 @@
             dscore = probs * (dot(v, dot_s[t, c]) - delta_s[t, c])
             pb = probs.astype(jnp.bfloat16)
             db = dscore.astype(jnp.bfloat16)
-            dkv_ref[k_rows, key_cols] += dot(db, qs[t, c])
-            dkv_ref[k_rows, val_cols] += dot(pb, dos[t, c])
+            dk = dot(db, qs[t, c])
+            dv = dot(pb, dos[t, c])
+            for j, span in enumerate(spans):
+                dkv_ref[span, key_cols] += dk[j * TILE : (j + 1) * TILE]
+                dkv_ref[span, val_cols] += dv[j * TILE : (j + 1) * TILE]
             kt = k.astype(jnp.float32).T.astype(jnp.bfloat16)
             dqt[t, c] += dot(kt, db)
 
     for t in range(q_tiles):
         own = first_tile + t
 
-        @pl.loop(0, own)
-        def _(k_tile):
-            @pl.when(mask_ref[own, k_tile] > 0)
-            def _():
-                pair(t, k_tile, None)
+        def note(k_tile, count):
+            needed_ref[count] = k_tile
+            return count + jnp.where(mask_ref[own, k_tile] > 0, 1, 0)
+
+        count = lax.fori_loop(0, own, note, jnp.int32(0))
+
+        @pl.loop(0, count // 2)
+        def _(i):
+            terms(t, (needed_ref[2 * i], needed_ref[2 * i + 1]), None)
 
         row = lax.broadcasted_iota(jnp.int32, (TILE, TILE), 0)
         col = lax.broadcasted_iota(jnp.int32, (TILE, TILE), 1)
         seg_k = segk_ref[t * TILE : (t + 1) * TILE, :]
         seg_q = segq_ref[:, t * TILE : (t + 1) * TILE]
         inner = jnp.where((row <= col) & (seg_k == seg_q), 1.0, 0.0)
-        inner = jnp.concatenate([inner] * GROUP, 1) > 0.5
-        pair(t, own, inner)
+        inner = jnp.concatenate([inner] * GROUP, 1)
+
+        @pl.when(lax.rem(count, 2) == 1)
+        def _():
+            whole = jnp.concatenate([jnp.ones_like(inner), inner], 0)
+            terms(t, (needed_ref[count - 1], own), whole > 0.5)
+
+        @pl.when(lax.rem(count, 2) == 0)
+        def _():
+            terms(t, (own,), inner > 0.5)
 
         rows = slice(t * TILE, (t + 1) * TILE)
         cosine = cos_ref[rows, :]
@@ -243,6 +267,7 @@
         scratch_shapes=[
             pltpu.VMEM((q_tiles, kv_local, 1, wide), jnp.float32),
             pltpu.VMEM((q_tiles, kv_local, HEAD_SIZE, wide), jnp.float32),
+            pltpu.SMEM((block_mask.shape[0],), jnp.int32),
         ],
         compiler_params=pltpu.CompilerParams(vmem_limit_bytes=ATTENTION_BYTES),
         name="attention",
@@ -253,11 +278,11 @@
 
 
 def project_kernel(
-    n_ctx, n, dq_ref, terms_ref, cos_ref, sin_ref, wq_ref, wk_ref, wv_ref, out_ref,
+    n_ctx, n, dq_hbm, terms_ref, cos_ref, sin_ref, wq_ref, wk_ref, wv_ref, out_ref,
     wq, wk, wv, acc, send, send_scale, recv, recv_scale,
-    dkv_ref, total, near, part, part_scale, far, far_scale,
+    dq_ref, dkv_ref, total, own, near, part, part_scale, far, far_scale,
     w_sem, send_sem, recv_sem, send_scale_sem, recv_scale_sem,
-    near_send_sem, near_sem, part_sem, far_sem, part_scale_sem, far_scale_sem,
+    dq_sem, own_sem, near_send_sem, near_sem, part_sem, far_sem, part_scale_sem, far_scale_sem,
 ):
     me = lax.axis_index("tp")
     chips = n_ctx // 2
@@ -359,6 +384,9 @@
     def token_rows(block):
         return pl.ds(pl.multiple_of(block * tokens, tokens), tokens)
 
+    def load_own(j):
+        return pltpu.make_async_copy(terms_ref.at[token_rows(2 * j + core), :], own.at[j], own_sem.at[j])
+
     def to_sibling(j):
         return pltpu.make_async_remote_copy(
             src_ref=terms_ref.at[token_rows(2 * j + 1 - core), :],
@@ -388,22 +416,26 @@
     @pl.loop(0, chip + 1)
     def _(j):
         to_sibling(j).start()
+        load_own(j).start()
+
+    pltpu.make_async_copy(dq_hbm, dq_ref, dq_sem.at[0]).start()
 
     @pl.loop(0, chip)
     def _(j):
+        load_own(j).wait()
         to_sibling(j).wait_recv()
         for r in range(8):
             rows = slice(r * group, (r + 1) * group)
-            at = pl.ds(pl.multiple_of((2 * j + core) * tokens + r * group, group), group)
-            x = terms_ref[at, :] + near[j, rows, :]
+            x = own[j, rows, :] + near[j, rows, :]
             largest = jnp.maximum(jnp.max(jnp.abs(x), axis=0, keepdims=True), 1e-30)
             part_scale[j, r : r + 1, :] = largest * (1.0 / 32767.0)
             part[j, rows, :] = jnp.round(x * (32767.0 / largest)).astype(jnp.int32).astype(jnp.int16)
         for copy in to_owner(chip, j):
             copy.start()
 
+    load_own(chip).wait()
     to_sibling(chip).wait_recv()
-    total[...] = terms_ref[token_rows(place), :] + near[chip]
+    total[...] = own[chip] + near[chip]
 
     @pl.loop(chip + 1, chips)
     def _(j):
@@ -420,6 +452,8 @@
         x = x * cos_ref[...] - pltpu.roll(x, HEAD_SIZE // 2, 1) * sin_ref[...]
         dkv_ref[:, cols] = x.astype(jnp.bfloat16)
     dkv_ref[:, kv_half:] = total[:, kv_half:].astype(jnp.bfloat16)
+
+    pltpu.make_async_copy(dq_hbm, dq_ref, dq_sem.at[0]).wait()
 
     @pl.loop(0, chip + 1)
     def _(j):
@@ -489,7 +523,7 @@
     return pl.pallas_call(
         functools.partial(project_kernel, n_ctx, n),
         out_shape=jax.ShapeDtypeStruct((chunk_rows, tokens), jnp.bfloat16),
-        in_specs=[vm, vm, vm, vm, hbm, hbm, hbm],
+        in_specs=[hbm, hbm, vm, vm, hbm, hbm, hbm],
         out_specs=vm,
         scratch_shapes=[
             pltpu.VMEM(w_query.shape, jnp.bfloat16),
@@ -500,8 +534,10 @@
             pltpu.VMEM((slots, 8, tokens), jnp.float32),
             pltpu.VMEM((2, slots, sub_rows, tokens), jnp.int16),
             pltpu.VMEM((2, slots, 8, tokens), jnp.float32),
+            pltpu.VMEM(dq.shape, jnp.bfloat16),
             pltpu.VMEM((tokens, kv_width), jnp.bfloat16),
             pltpu.VMEM((tokens, kv_width), jnp.float32),
+            pltpu.VMEM((chips, tokens, kv_width), jnp.float32),
             pltpu.VMEM((chips, tokens, kv_width), jnp.float32),
             pltpu.VMEM((chips, tokens, kv_width), jnp.int16),
             pltpu.VMEM((chips, 8, kv_width), jnp.float32),
@@ -513,7 +549,8 @@
             dma((slots,)),
             dma((2, slots)),
         ]
-        + [dma((chips,))] * 6,
+        + [dma((1,))]
+        + [dma((chips,))] * 7,
         compiler_params=pltpu.CompilerParams(
             collective_id=2, has_side_effects=True, vmem_limit_bytes=VMEM_BYTES
         ),

time: 111 us -> 110 us (level)
  the two profiles are of different devices: /device:TPU:18 before, /device:TPU:12 now
where the time goes in v3:
time: 110 us; the launch traced here: 109 us
  Pallas kernels  96.9 us (88%)
  local copies, waits for them, and re-layouts  10.8 us (10%)
  other arithmetic  1.37 us (1%)
    pallas_call x1, Pallas kernels, project(): pl.pallas_call(functools.partial(project_kernel, n_ctx, n), out_shape=jax...  76.2 us
    pallas_call x1, Pallas kernels, gather(): pl.pallas_call(functools.partial(gather_kernel, n), out_shape=(jax.ShapeD...  16.6 us
    unnamed x23, local copies, waits for them, and re-layouts  9.91 us
    pallas_call x1, Pallas kernels, attention(): pl.pallas_call(attention_kernel, out_shape=(jax.ShapeDtypeStruct((tokens,...  4.17 us

profile of v3, /device:TPU:12, one launch (start us, length us, event | category | flops | bytes accessed | tf_op | source)
XLA Modules:
  0.0 109.2 jit_solution(10048034539588074276)
XLA Ops:
  0.0 0.0 copy-start.10
  0.0 0.0 copy-start.9
  0.0 0.8 dynamic_slice.3
  0.8 0.7 convert_element_type.10
  1.5 0.1 copy.13.segk_ref
  1.6 0.5 fusion
  2.2 0.1 pad_maximum_fusion
  2.3 0.0 copy-start.1
  2.3 0.0 copy-start.2
  2.3 0.0 copy-start.4
  2.3 1.2 %copy-done.4 = bf16[256,1280]{1,0:T(8,128)(2,1)S(1)} copy-done((bf16[256,1280]{1,0:T(8,128)(2,1)S(1)}, bf16[256,1280]{1,0:T(8,128)(2,1)}, u32[]{:S(2)}) %copy-start.4) | copy-done | bytes 655384
  3.5 0.0 copy-start.5
  3.5 1.1 copy-done.5
  4.6 0.0 copy-start.6
  4.6 1.1 copy-done.6
  5.7 0.0 copy-start.7
  5.7 0.9 copy-done.7
  6.6 0.0 copy-start.8
  6.6 0.9 copy-done.8
  7.5 16.6 %gather.1 = (bf16[8,256,512]{2,1,0:T(8,128)(2,1)S(1)}, bf16[2,2,640,128]{3,2,1,0:T(8,128)(2,1)S(1)}, bf16[2,2,640,128]{3,2,1,0:T(8,128)(2,1)S(1)}, bf16[2,2,128,...) custom-call(bf16[256,256]{1,0:T(8,128)(2,1)S(1)} %copy-done.7, ...), custom_call_target="tpu_custom_call" | custom-call | tf_op jit(solution)/shard_map/gather/pallas_call | solution.py:157
  24.1 0.0 copy-done.10
  24.1 0.0 copy-done.9
  24.1 4.2 %attention.1 = (bf16[256,1280]{1,0:T(8,128)(2,1)S(1)}, f32[2048,512]{1,0:T(8,128)S(1)}) custom-call(s32[1]{0:T(128)} %bitcast.start_ref, s32[16,16]{1,0:T(8,128)S(1)} %copy-done.10, bf16[2,2,640,128]{3,2,1,0:T(8,128)(2,1)S(1)} %get-tuple-element.13.qs, bf16[2,2,640,128]{3,2,1,0:T(8,128)(2,1)S(1)} %get-tuple-element.14.dos, ...), custom_call_target="tpu_custom_call" | custom-call | tf_op jit(solution)/shard_map/attention/pallas_call | solution.py:259
  28.3 0.0 copy-done.1
  28.3 0.0 copy-done.2
  28.3 0.0 copy-start
  28.3 1.9 %copy-done = f32[2048,512]{1,0:T(8,128)} copy-done((f32[2048,512]{1,0:T(8,128)}, f32[2048,512]{1,0:T(8,128)S(1)}, u32[]{:S(2)}) %copy-start) | copy-done | bytes 4194328
  30.2 0.0 copy-start.3
  30.2 0.8 copy-done.3
  31.1 76.2 %project.1 = bf16[1280,256]{1,0:T(8,128)(2,1)} custom-call(bf16[256,1280]{1,0:T(8,128)(2,1)} %copy-done.3, f32[2048,512]{1,0:T(8,128)} %copy-done, f32[256,128]{1,0:T(8,128)} %copy-done.1, f32[256,128]{1,0:T(8,128)} %copy-done.2, bf16[5120,1280]{1,0:T(8,128)(2,1)} %wq_ref.1, bf16[5120,256]{1,0:T(8,128)(2,1)} %wk_ref.1, bf16[5120,256]{1,0:T(8,128)(2,1)} %wv_ref.1), custom_call_target="tpu_custom_call" | custom-call | tf_op jit(solution)/shard_map/project/pallas_call | solution.py:523
  107.2 2.0 %copy.15 = bf16[1280,256]{1,0:T(8,128)(2,1)} copy(bf16[1280,256]{1,0:T(8,128)(2,1)} %project.1) | data formatting | bytes 1310720
  (1 shorter events, 0.0 us)
Async XLA Ops:
  0.0 24.1 %copy-start.10 = (s32[16,16]{1,0:T(8,128)S(1)}, s32[16,16]{1,0:T(8,128)}, u32[]{:S(2)}) copy-start(s32[16,16]{1,0:T(8,128)} %mask_ref.1) | copy-start | bytes 3076
  0.0 24.1 %copy-start.9 = (f32[10,256]{1,0:T(8,128)S(1)}, f32[10,256]{1,0:T(8,128)}, u32[]{:S(2)}) copy-start(f32[10,256]{1,0:T(8,128)} %lse_ref.1) | copy-start | bytes 30724
  2.3 25.9 %copy-start.1 = (f32[256,128]{1,0:T(8,128)}, f32[256,128]{1,0:T(8,128)S(1)}, u32[]{:S(2)}) copy-start(f32[256,128]{1,0:T(8,128)S(1)} %get-tuple-element.24.cos_ref) | copy-start | bytes 393220
  2.3 25.9 %copy-start.2 = (f32[256,128]{1,0:T(8,128)}, f32[256,128]{1,0:T(8,128)S(1)}, u32[]{:S(2)}) copy-start(f32[256,128]{1,0:T(8,128)S(1)} %get-tuple-element.25.sin_ref) | copy-start | bytes 393220
  2.3 1.2 %copy-start.4 = (bf16[256,1280]{1,0:T(8,128)(2,1)S(1)}, bf16[256,1280]{1,0:T(8,128)(2,1)}, u32[]{:S(2)}) copy-start(bf16[256,1280]{1,0:T(8,128)(2,1)} %q_hbm.1) | copy-start | bytes 1966084
  3.5 1.1 copy-start.5
  4.6 1.1 copy-start.6
  5.7 0.9 copy-start.7
  6.6 0.9 copy-start.8
  28.3 1.9 %copy-start = (f32[2048,512]{1,0:T(8,128)}, f32[2048,512]{1,0:T(8,128)S(1)}, u32[]{:S(2)}) copy-start(f32[2048,512]{1,0:T(8,128)S(1)} %get-tuple-element.20.terms_ref) | copy-start | bytes 12582916
  30.2 0.8 copy-start.3

commit v4 on v3

--- a/solution.py
+++ b/solution.py
@@ -14,8 +14,8 @@
 GROUP = QUERY_HEADS // KEY_VALUE_HEADS
 SCALE = HEAD_SIZE ** (-0.5)
 MESH = pl.DeviceIdType.MESH
-VMEM_BYTES = 56 * 1024 * 1024
-ATTENTION_BYTES = 24 * 1024 * 1024
+PROJECT_BYTES = 60 * 1024 * 1024
+ATTENTION_BYTES = 56 * 1024 * 1024
 
 rope_base = 1000000.0
 
@@ -38,16 +38,10 @@
 
 
 def gather_kernel(
-    n, kp_ref, v_ref, q_hbm, do_hbm, ao_hbm, cos_ref, sin_ref,
+    n, kp_hbm, v_hbm, q_hbm, do_hbm, ao_hbm, cos_ref, sin_ref,
     kv_ref, qs_ref, dos_ref, qt_ref, dot_ref, delta_ref,
-    q_ref, do_ref, ao_ref, load_sem, send_sem, recv_sem, pass_sem, pass_recv_sem,
+    kp_ref, q_ref, do_ref, ao_ref, load_sem, send_sem, recv_sem, pass_sem, pass_recv_sem,
 ):
-    loads = [
-        pltpu.make_async_copy(src, dst, load_sem.at[j])
-        for j, (src, dst) in enumerate(((q_hbm, q_ref), (do_hbm, do_ref), (ao_hbm, ao_ref)))
-    ]
-    for copy in loads:
-        copy.start()
     me = lax.axis_index("ctx")
     chip, core = me // 2, lax.rem(me, 2)
     sibling = 2 * chip + 1 - core
@@ -55,6 +49,20 @@
     tokens, kv_cols = kp_ref.shape
     heads = q_ref.shape[1] // HEAD_SIZE
     q_tiles = tokens // TILE
+    loads = [
+        pltpu.make_async_copy(src, dst, load_sem.at[j])
+        for j, (src, dst) in enumerate(
+            (
+                (kp_hbm, kp_ref),
+                (v_hbm, kv_ref.at[me, :, pl.ds(kv_cols, kv_cols)]),
+                (q_hbm, q_ref),
+                (do_hbm, do_ref),
+                (ao_hbm, ao_ref),
+            )
+        )
+    ]
+    for copy in loads:
+        copy.start()
 
     barrier = pltpu.get_barrier_semaphore()
     for away in range(1, chips):
@@ -62,12 +70,13 @@
         pl.semaphore_signal(barrier, inc=1, device_id={"ctx": other}, device_id_type=MESH)
     pl.semaphore_signal(barrier, inc=1, device_id={"ctx": sibling}, device_id_type=MESH)
 
+    loads[0].wait()
     for c in range(kv_cols // HEAD_SIZE):
         cols = slice(c * HEAD_SIZE, (c + 1) * HEAD_SIZE)
         x = kp_ref[:, cols].astype(jnp.float32)
         x = x * cos_ref[...] + pltpu.roll(x, HEAD_SIZE // 2, 1) * sin_ref[...]
         kv_ref[me, :, cols] = x.astype(jnp.bfloat16)
-    kv_ref[me, :, kv_cols:] = v_ref[...]
+    loads[1].wait()
 
     def direct(source, target):
         slot = 2 * source + core
@@ -99,7 +108,7 @@
             direct(chip, jnp.minimum(chip + away, chips - 1)).start()
 
     handed(chip, core).start()
-    for copy in loads:
+    for copy in loads[2:]:
         copy.wait()
 
     @pl.loop(0, q_tiles * heads)
@@ -150,7 +159,7 @@
     q_tiles = tokens // TILE
     wide = GROUP * TILE
     vm = pl.BlockSpec(memory_space=pltpu.VMEM)
-    hbm = pl.BlockSpec(memory_space=pl.ANY)
+    hbm = pl.BlockSpec(memory_space=pltpu.HBM)
     dma = pltpu.SemaphoreType.DMA
     stacked = jax.ShapeDtypeStruct((q_tiles, kv_local, wide, HEAD_SIZE), jnp.bfloat16)
     turned = jax.ShapeDtypeStruct((q_tiles, kv_local, HEAD_SIZE, wide), jnp.bfloat16)
@@ -164,9 +173,12 @@
             turned,
             jax.ShapeDtypeStruct((q_tiles, kv_local, 1, wide), jnp.float32),
         ),
-        in_specs=[vm, vm, hbm, hbm, hbm, vm, vm],
+        in_specs=[hbm] * 5 + [vm, vm],
         out_specs=(vm,) * 6,
-        scratch_shapes=[pltpu.VMEM(query.shape, jnp.bfloat16)] * 3 + [dma((3,))] + [dma((n // 2,))] * 4,
+        scratch_shapes=[pltpu.VMEM(key_projected.shape, jnp.bfloat16)]
+        + [pltpu.VMEM(query.shape, jnp.bfloat16)] * 3
+        + [dma((5,))]
+        + [dma((n // 2,))] * 4,
         compiler_params=pltpu.CompilerParams(
             collective_id=1, has_side_effects=True, vmem_limit_bytes=ATTENTION_BYTES
         ),
@@ -552,7 +564,7 @@
         + [dma((1,))]
         + [dma((chips,))] * 7,
         compiler_params=pltpu.CompilerParams(
-            collective_id=2, has_side_effects=True, vmem_limit_bytes=VMEM_BYTES
+            collective_id=2, has_side_effects=True, vmem_limit_bytes=PROJECT_BYTES
         ),
         name="project",
     )(dq, terms, cosine, sine, w_query, key_weight, value_weight)

time: 110 us -> 109 us (level)
  local copies, waits for them, and re-layouts: 10.8 us -> 3.53 us
  Pallas kernels: 96.9 us -> 103 us
    unnamed x23 -> x3, local copies, waits for them, and re-layouts: 9.91 us -> 1.97 us
    pallas_call x1, Pallas kernels: 4.17 us -> 7.77 us  [attention(): pl.pallas_call(attention_kernel, out_shape=(jax.ShapeDtypeStruct((tokens,...]
    pallas_call x1, Pallas kernels: 16.6 us -> 19.1 us  [gather(): pl.pallas_call(functools.partial(gather_kernel, n), out_shape=(jax.ShapeD...]
where the time goes in v4:
time: 109 us
  Pallas kernels  103 us (94%)
  local copies, waits for them, and re-layouts  3.53 us (3%)
  other arithmetic  2.09 us (2%)
    pallas_call x1, Pallas kernels, project(): pl.pallas_call(functools.partial(project_kernel, n_ctx, n), out_shape=jax...  76.1 us
    pallas_call x1, Pallas kernels, gather(): pl.pallas_call(functools.partial(gather_kernel, n), out_shape=(jax.ShapeD...  19.1 us
    pallas_call x1, Pallas kernels, attention(): pl.pallas_call(attention_kernel, out_shape=(jax.ShapeDtypeStruct((tokens,...  7.77 us

profile of v4, /device:TPU:12, one launch (start us, length us, event | category | flops | bytes accessed | tf_op | source)
XLA Modules:
  0.0 108.6 jit_solution(6687811629741526589)
XLA Ops:
  0.0 0.8 dynamic_slice.3
  0.8 0.0 copy-start
  0.8 0.7 convert_element_type.10
  1.5 0.8 copy.13.segk_ref
  2.3 0.5 fusion
  2.8 0.9 pad_maximum_fusion
  3.7 19.1 %gather.1 = (bf16[8,256,512]{2,1,0:T(8,128)(2,1)}, bf16[2,2,640,128]{3,2,1,0:T(8,128)(2,1)}, bf16[2,2,640,128]{3,2,1,0:T(8,128)(2,1)}, bf16[2,2,128,640]{3,2,1,0...) custom-call(bf16[256,256]{1,0:T(8,128)(2,1)} %kp_hbm.1, bf16[256,256]{1,0:T(8,128)(2,1)} %v_hbm.1, ...), custom_call_target="tpu_custom_call" | custom-call | tf_op jit(solution)/shard_map/gather/pallas_call | solution.py:166
  22.7 0.0 copy-done
  22.8 7.8 %attention.1 = (bf16[256,1280]{1,0:T(8,128)(2,1)}, f32[2048,512]{1,0:T(8,128)}) custom-call(s32[1]{0:T(128)} %bitcast.start_ref, s32[16,16]{1,0:T(8,128)} %mask_ref.1, bf16[2,2,640,128]{3,2,1,0:T(8,128)(2,1)} %get-tuple-element.13.qs, bf16[2,2,640,128]{3,2,1,0:T(8,128)(2,1)} %get-tuple-element.14.dos, bf16[2,2,128,640]{3,2,1,0:T(8,128)(2,1)} %get-tuple-element.15.qt_s, ...), custom_call_target="tpu_custom_call" | custom-call | tf_op jit(solution)/shard_map/attention/pallas_call | solution.py:271
  30.5 76.1 %project.1 = bf16[1280,256]{1,0:T(8,128)(2,1)} custom-call(bf16[256,1280]{1,0:T(8,128)(2,1)} %get-tuple-element.19.dq_hbm, f32[2048,512]{1,0:T(8,128)} %get-tuple-element.20.terms_ref, f32[256,128]{1,0:T(8,128)} %get-tuple-element.24.cos_ref, f32[256,128]{1,0:T(8,128)} %get-tuple-element.25.sin_ref, bf16[5120,1280]{1,0:T(8,128)(2,1)} %wq_ref.1, ...), custom_call_target="tpu_custom_call" | custom-call | tf_op jit(solution)/shard_map/project/pallas_call | solution.py:535
  106.6 2.0 %copy.15 = bf16[1280,256]{1,0:T(8,128)(2,1)} copy(bf16[1280,256]{1,0:T(8,128)(2,1)} %project.1) | data formatting | bytes 1310720
  (1 shorter events, 0.0 us)
Async XLA Ops:
  0.8 22.0 %copy-start = (s32[256]{0:T(256)}, s32[256]{0:T(256)S(1)}, u32[]{:S(2)}) copy-start(s32[256]{0:T(256)S(1)} %dynamic_slice.3) | copy-start | bytes 3076

commit v5 on v4

--- a/solution.py
+++ b/solution.py
@@ -37,10 +37,18 @@
     return lax.dot_general(a, b, (dims, ((), ())), preferred_element_type=jnp.float32)
 
 
+def line_ends(at, n):
+    is_end = (at == 0) | (at == n - 1)
+    is_next = (at == 1) | (at == n - 2)
+    mate = jnp.where(at == 0, 1, jnp.where(at == n - 1, n - 2, jnp.where(at == 1, 0, n - 1)))
+    return is_end, is_next, mate
+
+
 def gather_kernel(
-    n, kp_hbm, v_hbm, q_hbm, do_hbm, ao_hbm, cos_ref, sin_ref,
-    kv_ref, qs_ref, dos_ref, qt_ref, dot_ref, delta_ref,
-    kp_ref, q_ref, do_ref, ao_ref, load_sem, send_sem, recv_sem, pass_sem, pass_recv_sem,
+    n, n_tp, kp_hbm, v_hbm, q_hbm, do_hbm, ao_hbm, cos_ref, sin_ref, wk_hbm, wv_hbm,
+    kv_ref, qs_ref, dos_ref, qt_ref, dot_ref, delta_ref, far_ref,
+    kp_ref, q_ref, do_ref, ao_ref, load_sem, far_send_sem, far_recv_sem,
+    send_sem, recv_sem, pass_sem, pass_recv_sem,
 ):
     me = lax.axis_index("ctx")
     chip, core = me // 2, lax.rem(me, 2)
@@ -70,6 +78,30 @@
         pl.semaphore_signal(barrier, inc=1, device_id={"ctx": other}, device_id_type=MESH)
     pl.semaphore_signal(barrier, inc=1, device_id={"ctx": sibling}, device_id_type=MESH)
 
+    line = lax.axis_index("tp")
+    is_end, is_next, mate = line_ends(line, n_tp)
+    half = far_ref.shape[1] // 2
+    chunk = jnp.where(line == 0, n_tp - 1, 0)
+
+    def far_weights():
+        rows = pl.ds(pl.multiple_of(chunk * 2 * half + core * half, half), half)
+        there = pl.ds(pl.multiple_of(core * half, half), half)
+        return [
+            pltpu.make_async_remote_copy(
+                src_ref=src.at[rows, :],
+                dst_ref=far_ref.at[j, there, :],
+                send_sem=far_send_sem.at[j],
+                recv_sem=far_recv_sem.at[j],
+                device_id={"tp": mate},
+                device_id_type=MESH,
+            )
+            for j, src in enumerate((wk_hbm, wv_hbm))
+        ]
+
+    @pl.when(is_end | is_next)
+    def _():
+        pl.semaphore_signal(barrier, inc=1, device_id={"tp": mate}, device_id_type=MESH)
+
     loads[0].wait()
     for c in range(kv_cols // HEAD_SIZE):
         cols = slice(c * HEAD_SIZE, (c + 1) * HEAD_SIZE)
@@ -100,7 +132,7 @@
             device_id_type=MESH,
         )
 
-    pl.semaphore_wait(barrier, chips)
+    pl.semaphore_wait(barrier, chips + jnp.where(is_end | is_next, 1, 0))
     for away in range(chips - 1, 0, -1):
 
         @pl.when(chip + away < chips)
@@ -108,6 +140,12 @@
             direct(chip, jnp.minimum(chip + away, chips - 1)).start()
 
     handed(chip, core).start()
+
+    @pl.when(is_end)
+    def _():
+        for copy in far_weights():
+            copy.start()
+
     for copy in loads[2:]:
         copy.wait()
 
@@ -152,8 +190,18 @@
         def _():
             direct(chip, jnp.minimum(chip + away, chips - 1)).wait_send()
 
-
-def gather(n, key_projected, value, query, grad, attention_output, cosine, sine):
+    @pl.when(is_next)
+    def _():
+        for copy in far_weights():
+            copy.wait_recv()
+
+    @pl.when(is_end)
+    def _():
+        for copy in far_weights():
+            copy.wait_send()
+
+
+def gather(n, n_tp, key_projected, value, query, grad, attention_output, cosine, sine, key_weight, value_weight):
     tokens, kv_cols = key_projected.shape
     kv_local = kv_cols // HEAD_SIZE
     q_tiles = tokens // TILE
@@ -164,7 +212,7 @@
     stacked = jax.ShapeDtypeStruct((q_tiles, kv_local, wide, HEAD_SIZE), jnp.bfloat16)
     turned = jax.ShapeDtypeStruct((q_tiles, kv_local, HEAD_SIZE, wide), jnp.bfloat16)
     return pl.pallas_call(
-        functools.partial(gather_kernel, n),
+        functools.partial(gather_kernel, n, n_tp),
         out_shape=(
             jax.ShapeDtypeStruct((n, tokens, 2 * kv_cols), jnp.bfloat16),
             stacked,
@@ -172,18 +220,19 @@
             turned,
             turned,
             jax.ShapeDtypeStruct((q_tiles, kv_local, 1, wide), jnp.float32),
+            jax.ShapeDtypeStruct((2, key_weight.shape[0] // n_tp, kv_cols), jnp.bfloat16),
         ),
-        in_specs=[hbm] * 5 + [vm, vm],
-        out_specs=(vm,) * 6,
+        in_specs=[hbm] * 5 + [vm, vm, hbm, hbm],
+        out_specs=(vm,) * 6 + (pl.BlockSpec(memory_space=pl.ANY),),
         scratch_shapes=[pltpu.VMEM(key_projected.shape, jnp.bfloat16)]
         + [pltpu.VMEM(query.shape, jnp.bfloat16)] * 3
-        + [dma((5,))]
+        + [dma((5,)), dma((2,)), dma((2,))]
         + [dma((n // 2,))] * 4,
         compiler_params=pltpu.CompilerParams(
             collective_id=1, has_side_effects=True, vmem_limit_bytes=ATTENTION_BYTES
         ),
         name="gather",
-    )(key_projected, value, query, grad, attention_output, cosine, sine)
+    )(key_projected, value, query, grad, attention_output, cosine, sine, key_weight, value_weight)
 
 
 def attention_kernel(
@@ -290,11 +339,11 @@
 
 
 def project_kernel(
-    n_ctx, n, dq_hbm, terms_ref, cos_ref, sin_ref, wq_ref, wk_ref, wv_ref, out_ref,
+    n_ctx, n, dq_hbm, terms_ref, cos_ref, sin_ref, wq_ref, wk_ref, wv_ref, far_hbm, out_ref,
     wq, wk, wv, acc, send, send_scale, recv, recv_scale,
-    dq_ref, dkv_ref, total, own, near, part, part_scale, far, far_scale,
+    far_w, far_dkv, dq_ref, dkv_ref, total, own, near, part, part_scale, far, far_scale,
     w_sem, send_sem, recv_sem, send_scale_sem, recv_scale_sem,
-    dq_sem, own_sem, near_send_sem, near_sem, part_sem, far_sem, part_scale_sem, far_scale_sem,
+    far_load_sem, far_send_sem, far_recv_sem, raw_sem, dq_sem, own_sem, near_send_sem, near_sem, part_sem, far_sem, part_scale_sem, far_scale_sem,
 ):
     me = lax.axis_index("tp")
     chips = n_ctx // 2
@@ -308,6 +357,7 @@
     sub_rows = acc.shape[0]
     subs = chunk_rows // sub_rows
     steps = 2 * (n - 1) * subs
+    is_end, is_next, mate = line_ends(me, n)
 
     def plan(i):
         way = lax.rem(i, 2)
@@ -316,7 +366,10 @@
         step = i // (2 * subs)
         chunk = jnp.where(rightward == 1, n - 1 - step, step)
         active = jnp.where(rightward == 1, chunk > me, chunk < me)
-        return rightward, chunk, sub, active
+        early = active & is_end & (step == 0)
+        late = active & jnp.logical_not(early)
+        joined = is_next & (step == 0) & (rightward == jnp.where(me == 1, 1, 0))
+        return rightward, chunk, sub, early, late, joined
 
     def weight_copies(chunk, sub):
         at = chunk * subs + sub
@@ -362,11 +415,18 @@
         scale = recv_scale[rightward, slot, 0:1, :]
         acc[...] += recv[rightward, slot].astype(jnp.int32).astype(jnp.float32) * scale
 
+    dq_load = pltpu.make_async_copy(dq_hbm, dq_ref, dq_sem.at[0])
+    dq_load.start()
+
     @pl.loop(0, steps)
     def _(i):
-        _, chunk, sub, active = plan(i)
-
-        @pl.when(active)
+        _, chunk, sub, early, late, _ = plan(i)
+
+        @pl.when(early)
+        def _():
+            weight_copies(chunk, sub)[0].start()
+
+        @pl.when(late)
         def _():
             for copy in weight_copies(chunk, sub):
                 copy.start()
@@ -430,7 +490,59 @@
         to_sibling(j).start()
         load_own(j).start()
 
-    pltpu.make_async_copy(dq_hbm, dq_ref, dq_sem.at[0]).start()
+    far_half = far_w.shape[1] // 2
+    mine = pl.ds(pl.multiple_of(core * far_half, far_half), far_half)
+    far_loads = [
+        pltpu.make_async_copy(far_hbm.at[j, mine, :], far_w.at[j, mine, :], far_load_sem.at[j])
+        for j in range(2)
+    ]
+    far_sends = [
+        pltpu.make_async_remote_copy(
+            src_ref=far_hbm.at[j, mine, :],
+            dst_ref=far_w.at[j, mine, :],
+            send_sem=far_send_sem.at[j],
+            recv_sem=far_recv_sem.at[j],
+            device_id={"ctx": sibling},
+            device_id_type=MESH,
+        )
+        for j in range(2)
+    ]
+    raw = pltpu.make_async_remote_copy(
+        src_ref=dkv_ref,
+        dst_ref=far_dkv,
+        send_sem=raw_sem.at[0],
+        recv_sem=raw_sem.at[1],
+        device_id={"tp": mate},
+        device_id_type=MESH,
+    )
+
+    @pl.when(is_next)
+    def _():
+        for copy in far_loads + far_sends:
+            copy.start()
+
+    def send_coded(rightward, chunk, sub):
+        slot = chunk * subs + sub
+        largest = jnp.maximum(jnp.max(jnp.abs(acc[...]), axis=0, keepdims=True), 1e-30)
+        send_scale[slot] = jnp.broadcast_to(largest * (1.0 / 32767.0), send_scale.shape[1:])
+        coded = jnp.round(acc[...] * (32767.0 / largest))
+        send[slot] = coded.astype(jnp.int32).astype(jnp.int16)
+        for copy in remote(rightward, chunk, sub):
+            copy.start()
+
+    def query_parts(first, last):
+        @pl.when(is_end)
+        def _():
+            @pl.loop(first, last)
+            def _(sub):
+                chunk = jnp.where(me == 0, n - 1, 0)
+                weight_copies(chunk, sub)[0].wait()
+                rows = pl.ds(pl.multiple_of((chunk * subs + sub) * sub_rows, sub_rows), sub_rows)
+                acc[...] = dot(wq[rows, :], dq_ref[...], ((1,), (1,)))
+                send_coded(jnp.where(me == 0, 1, 0), chunk, sub)
+
+    dq_load.wait()
+    query_parts(0, subs // 2)
 
     @pl.loop(0, chip)
     def _(j):
@@ -445,6 +557,7 @@
         for copy in to_owner(chip, j):
             copy.start()
 
+    query_parts(subs // 2, subs)
     load_own(chip).wait()
     to_sibling(chip).wait_recv()
     total[...] = own[chip] + near[chip]
@@ -465,7 +578,18 @@
         dkv_ref[:, cols] = x.astype(jnp.bfloat16)
     dkv_ref[:, kv_half:] = total[:, kv_half:].astype(jnp.bfloat16)
 
-    pltpu.make_async_copy(dq_hbm, dq_ref, dq_sem.at[0]).wait()
+    @pl.when(is_end)
+    def _():
+        raw.start()
+
+    @pl.when(is_next)
+    def _():
+        for copy in far_loads:
+            copy.wait()
+        for copy in far_sends:
+            copy.wait_recv()
+            copy.wait_send()
+        raw.wait_recv()
 
     @pl.loop(0, chip + 1)
     def _(j):
@@ -478,9 +602,9 @@
 
     @pl.loop(0, steps)
     def _(i):
-        rightward, chunk, sub, active = plan(i)
-
-        @pl.when(active)
+        rightward, chunk, sub, _, late, joined = plan(i)
+
+        @pl.when(late)
         def _():
             own_term(chunk, sub)
 
@@ -488,13 +612,13 @@
             def _():
                 add_received(rightward, chunk, sub)
 
-            slot = chunk * subs + sub
-            largest = jnp.maximum(jnp.max(jnp.abs(acc[...]), axis=0, keepdims=True), 1e-30)
-            send_scale[slot] = jnp.broadcast_to(largest * (1.0 / 32767.0), send_scale.shape[1:])
-            coded = jnp.round(acc[...] * (32767.0 / largest))
-            send[slot] = coded.astype(jnp.int32).astype(jnp.int16)
-            for copy in remote(rightward, chunk, sub):
-                copy.start()
+            @pl.when(joined)
+            def _():
+                rows = pl.ds(pl.multiple_of(sub * sub_rows, sub_rows), sub_rows)
+                extra = dot(far_w[0, rows, :], far_dkv[:, :kv_half], ((1,), (1,)))
+                acc[...] += extra + dot(far_w[1, rows, :], far_dkv[:, kv_half:], ((1,), (1,)))
+
+            send_coded(rightward, chunk, sub)
 
     @pl.loop(0, subs)
     def _(sub):
@@ -513,15 +637,19 @@
 
     @pl.loop(0, steps)
     def _(i):
-        rightward, chunk, sub, active = plan(i)
-
-        @pl.when(active)
+        rightward, chunk, sub, early, late, _ = plan(i)
+
+        @pl.when(early | late)
         def _():
             for copy in remote(rightward, chunk, sub):
                 copy.wait_send()
 
-
-def project(n_ctx, n, dq, terms, cosine, sine, w_query, key_weight, value_weight):
+    @pl.when(is_end)
+    def _():
+        raw.wait_send()
+
+
+def project(n_ctx, n, dq, terms, cosine, sine, w_query, key_weight, value_weight, far_weight):
     tokens = dq.shape[0]
     kv_width = terms.shape[1]
     chips = n_ctx // 2
@@ -535,7 +663,7 @@
     return pl.pallas_call(
         functools.partial(project_kernel, n_ctx, n),
         out_shape=jax.ShapeDtypeStruct((chunk_rows, tokens), jnp.bfloat16),
-        in_specs=[hbm, hbm, vm, vm, hbm, hbm, hbm],
+        in_specs=[hbm, hbm, vm, vm, hbm, hbm, hbm, hbm],
         out_specs=vm,
         scratch_shapes=[
             pltpu.VMEM(w_query.shape, jnp.bfloat16),
@@ -546,6 +674,8 @@
             pltpu.VMEM((slots, 8, tokens), jnp.float32),
             pltpu.VMEM((2, slots, sub_rows, tokens), jnp.int16),
             pltpu.VMEM((2, slots, 8, tokens), jnp.float32),
+            pltpu.VMEM(far_weight.shape, jnp.bfloat16),
+            pltpu.VMEM((tokens, kv_width), jnp.bfloat16),
             pltpu.VMEM(dq.shape, jnp.bfloat16),
             pltpu.VMEM((tokens, kv_width), jnp.bfloat16),
             pltpu.VMEM((tokens, kv_width), jnp.float32),
@@ -561,13 +691,14 @@
             dma((slots,)),
             dma((2, slots)),
         ]
+        + [dma((2,))] * 4
         + [dma((1,))]
         + [dma((chips,))] * 7,
         compiler_params=pltpu.CompilerParams(
             collective_id=2, has_side_effects=True, vmem_limit_bytes=PROJECT_BYTES
         ),
         name="project",
-    )(dq, terms, cosine, sine, w_query, key_weight, value_weight)
+    )(dq, terms, cosine, sine, w_query, key_weight, value_weight, far_weight)
 
 
 def local(
@@ -589,8 +720,9 @@
     tok_rows = query.shape[0]
     q_start = lax.axis_index("ctx") * tok_rows
     cosine, sine = rope_tables(positions, HEAD_SIZE)
-    kv_blocks, *prepared = gather(
-        n_ctx, key_projected, value, query, output_gradient, attention_output, cosine, sine
+    kv_blocks, *prepared, far_weight = gather(
+        n_ctx, n_tp, key_projected, value, query, output_gradient, attention_output, cosine, sine,
+        key_weight, value_weight,
     )
     kv_whole = kv_blocks.reshape(n_ctx * tok_rows, kv_blocks.shape[-1])
     seg_row = lax.dynamic_slice_in_dim(segments, q_start, tok_rows).reshape(1, tok_rows)
@@ -598,7 +730,9 @@
     query_grad, terms = attention(
         first_tile, block_mask, prepared, lse, cosine, sine, kv_whole, seg_row
     )
-    return project(n_ctx, n_tp, query_grad, terms, cosine, sine, w_query, key_weight, value_weight)
+    return project(
+        n_ctx, n_tp, query_grad, terms, cosine, sine, w_query, key_weight, value_weight, far_weight
+    )
 
 
 def solution(mesh):

time: 109 us -> 113 us (1.037)
  Pallas kernels: 103 us -> 107 us
    pallas_call x1, Pallas kernels: 76.1 us -> 78.9 us  [project(): pl.pallas_call(functools.partial(project_kernel, n_ctx, n), out_shape=jax...]
    pallas_call x1, Pallas kernels: 19.1 us -> 20.3 us  [gather(): pl.pallas_call(functools.partial(gather_kernel, n, n_tp), out_shape=(jax....]
where the time goes in v5:
time: 113 us
  Pallas kernels  107 us (95%)
  local copies, waits for them, and re-layouts  3.52 us (3%)
  other arithmetic  2.06 us (2%)
    pallas_call x1, Pallas kernels, project(): pl.pallas_call(functools.partial(project_kernel, n_ctx, n), out_shape=jax...  78.9 us
    pallas_call x1, Pallas kernels, gather(): pl.pallas_call(functools.partial(gather_kernel, n, n_tp), out_shape=(jax....  20.3 us
    pallas_call x1, Pallas kernels, attention(): pl.pallas_call(attention_kernel, out_shape=(jax.ShapeDtypeStruct((tokens,...  7.77 us

profile of v5, /device:TPU:12, one launch (start us, length us, event | category | flops | bytes accessed | tf_op | source)
XLA Modules:
  0.0 112.5 jit_solution(12687699780784164239)
XLA Ops:
  0.0 0.8 dynamic_slice.3
  0.8 0.0 copy-start
  0.8 0.7 convert_element_type.10
  1.5 0.8 copy.13.segk_ref
  2.2 0.5 fusion
  2.8 0.8 pad_maximum_fusion
  3.6 20.3 %gather.1 = (bf16[8,256,512]{2,1,0:T(8,128)(2,1)}, bf16[2,2,640,128]{3,2,1,0:T(8,128)(2,1)}, bf16[2,2,640,128]{3,2,1,0:T(8,128)(2,1)}, bf16[2,2,128,640]{3,2,1,0...) custom-call(bf16[256,256]{1,0:T(8,128)(2,1)} %kp_hbm.1, ...), custom_call_target="tpu_custom_call" | custom-call | tf_op jit(solution)/shard_map/gather/pallas_call | solution.py:214
  23.9 0.0 copy-done
  23.9 7.8 %attention.1 = (bf16[256,1280]{1,0:T(8,128)(2,1)}, f32[2048,512]{1,0:T(8,128)}) custom-call(s32[1]{0:T(128)} %bitcast.start_ref, s32[16,16]{1,0:T(8,128)} %mask_ref.1, bf16[2,2,640,128]{3,2,1,0:T(8,128)(2,1)} %get-tuple-element.14.qs, bf16[2,2,640,128]{3,2,1,0:T(8,128)(2,1)} %get-tuple-element.15.dos, bf16[2,2,128,640]{3,2,1,0:T(8,128)(2,1)} %get-tuple-element.16.qt_s, ...), custom_call_target="tpu_custom_call" | custom-call | tf_op jit(solution)/shard_map/attention/pallas_call | solution.py:320
  31.7 78.9 %project.1 = bf16[1280,256]{1,0:T(8,128)(2,1)} custom-call(bf16[256,1280]{1,0:T(8,128)(2,1)} %get-tuple-element.20.dq_hbm, f32[2048,512]{1,0:T(8,128)} %get-tuple-element.21.terms_ref, f32[256,128]{1,0:T(8,128)} %get-tuple-element.26.cos_ref, f32[256,128]{1,0:T(8,128)} %get-tuple-element.27.sin_ref, bf16[5120,1280]{1,0:T(8,128)(2,1)} %wq_ref.1, ...), custom_call_target="tpu_custom_call" | custom-call | tf_op jit(solution)/shard_map/project/pallas_call | solution.py:663
  110.6 2.0 %copy.15 = bf16[1280,256]{1,0:T(8,128)(2,1)} copy(bf16[1280,256]{1,0:T(8,128)(2,1)} %project.1) | data formatting | bytes 1310720
  (1 shorter events, 0.0 us)
Async XLA Ops:
  0.8 23.1 %copy-start = (s32[256]{0:T(256)}, s32[256]{0:T(256)S(1)}, u32[]{:S(2)}) copy-start(s32[256]{0:T(256)S(1)} %dynamic_slice.3) | copy-start | bytes 3076

commit v6 on v5

--- a/solution.py
+++ b/solution.py
@@ -341,7 +341,7 @@
 def project_kernel(
     n_ctx, n, dq_hbm, terms_ref, cos_ref, sin_ref, wq_ref, wk_ref, wv_ref, far_hbm, out_ref,
     wq, wk, wv, acc, send, send_scale, recv, recv_scale,
-    far_w, far_dkv, dq_ref, dkv_ref, total, own, near, part, part_scale, far, far_scale,
+    far_w, far_dkv, dq_ref, dq_turned, query_part, dkv_ref, total, own, near, part, part_scale, far, far_scale,
     w_sem, send_sem, recv_sem, send_scale_sem, recv_scale_sem,
     far_load_sem, far_send_sem, far_recv_sem, raw_sem, dq_sem, own_sem, near_send_sem, near_sem, part_sem, far_sem, part_scale_sem, far_scale_sem,
 ):
@@ -350,7 +350,7 @@
     place = lax.axis_index("ctx")
     chip, core = place // 2, lax.rem(place, 2)
     sibling = 2 * chip + 1 - core
-    tokens, kv_width = dkv_ref.shape
+    kv_width, tokens = dkv_ref.shape
     kv_half = kv_width // 2
     group = tokens // 8
     chunk_rows = out_ref.shape[0]
@@ -398,15 +398,13 @@
         ]
 
     def own_term(chunk, sub):
-        for copy in weight_copies(chunk, sub):
+        for copy in weight_copies(chunk, sub)[1:]:
             copy.wait()
         at = chunk * subs + sub
         rows = pl.ds(pl.multiple_of(at * sub_rows, sub_rows), sub_rows)
         half = wk.shape[1]
-        contract = ((1,), (1,))
-        total = dot(wq[rows, :], dq_ref[...], contract)
-        total = total + dot(wk[rows, :], dkv_ref[:, :half], contract)
-        acc[...] = total + dot(wv[rows, :], dkv_ref[:, half:], contract)
+        term = query_part[rows, :] + dot(wk[rows, :], dkv_ref[:half, :])
+        acc[...] = term + dot(wv[rows, :], dkv_ref[half:, :])
 
     def add_received(rightward, chunk, sub):
         for copy in remote(rightward, chunk, sub):
@@ -538,10 +536,21 @@
                 chunk = jnp.where(me == 0, n - 1, 0)
                 weight_copies(chunk, sub)[0].wait()
                 rows = pl.ds(pl.multiple_of((chunk * subs + sub) * sub_rows, sub_rows), sub_rows)
-                acc[...] = dot(wq[rows, :], dq_ref[...], ((1,), (1,)))
+                acc[...] = dot(wq[rows, :], dq_turned[...])
                 send_coded(jnp.where(me == 0, 1, 0), chunk, sub)
 
+    def own_query(chunk, sub):
+        weight_copies(chunk, sub)[0].wait()
+        rows = pl.ds(pl.multiple_of((chunk * subs + sub) * sub_rows, sub_rows), sub_rows)
+        query_part[rows, :] = dot(wq[rows, :], dq_turned[...])
+
     dq_load.wait()
+
+    @pl.loop(0, dq_ref.shape[1] // HEAD_SIZE)
+    def _(h):
+        cols = pl.ds(pl.multiple_of(h * HEAD_SIZE, HEAD_SIZE), HEAD_SIZE)
+        dq_turned[cols, :] = dq_ref[:, cols].astype(jnp.float32).T.astype(jnp.bfloat16)
+
     query_parts(0, subs // 2)
 
     @pl.loop(0, chip)
@@ -558,6 +567,19 @@
             copy.start()
 
     query_parts(subs // 2, subs)
+
+    @pl.loop(0, steps)
+    def _(i):
+        _, chunk, sub, _, late, _ = plan(i)
+
+        @pl.when(late)
+        def _():
+            own_query(chunk, sub)
+
+    @pl.loop(0, subs)
+    def _(sub):
+        own_query(me, sub)
+
     load_own(chip).wait()
     to_sibling(chip).wait_recv()
     total[...] = own[chip] + near[chip]
@@ -575,8 +597,9 @@
         cols = slice(c * HEAD_SIZE, (c + 1) * HEAD_SIZE)
         x = total[:, cols] * SCALE
         x = x * cos_ref[...] - pltpu.roll(x, HEAD_SIZE // 2, 1) * sin_ref[...]
-        dkv_ref[:, cols] = x.astype(jnp.bfloat16)
-    dkv_ref[:, kv_half:] = total[:, kv_half:].astype(jnp.bfloat16)
+        dkv_ref[cols, :] = x.T.astype(jnp.bfloat16)
+        v_cols = slice(kv_half + c * HEAD_SIZE, kv_half + (c + 1) * HEAD_SIZE)
+        dkv_ref[v_cols, :] = total[:, v_cols].T.astype(jnp.bfloat16)
 
     @pl.when(is_end)
     def _():
@@ -615,8 +638,8 @@
             @pl.when(joined)
             def _():
                 rows = pl.ds(pl.multiple_of(sub * sub_rows, sub_rows), sub_rows)
-                extra = dot(far_w[0, rows, :], far_dkv[:, :kv_half], ((1,), (1,)))
-                acc[...] += extra + dot(far_w[1, rows, :], far_dkv[:, kv_half:], ((1,), (1,)))
+                extra = dot(far_w[0, rows, :], far_dkv[:kv_half, :])
+                acc[...] += extra + dot(far_w[1, rows, :], far_dkv[kv_half:, :])
 
             send_coded(rightward, chunk, sub)
 
@@ -675,9 +698,11 @@
             pltpu.VMEM((2, slots, sub_rows, tokens), jnp.int16),
             pltpu.VMEM((2, slots, 8, tokens), jnp.float32),
             pltpu.VMEM(far_weight.shape, jnp.bfloat16),
-            pltpu.VMEM((tokens, kv_width), jnp.bfloat16),
+            pltpu.VMEM((kv_width, tokens), jnp.bfloat16),
             pltpu.VMEM(dq.shape, jnp.bfloat16),
-            pltpu.VMEM((tokens, kv_width), jnp.bfloat16),
+            pltpu.VMEM(dq.shape[::-1], jnp.bfloat16),
+            pltpu.VMEM((width, tokens), jnp.float32),
+            pltpu.VMEM((kv_width, tokens), jnp.bfloat16),
             pltpu.VMEM((tokens, kv_width), jnp.float32),
             pltpu.VMEM((chips, tokens, kv_width), jnp.float32),
             pltpu.VMEM((chips, tokens, kv_width), jnp.float32),

time: 113 us -> 112 us (level)
    pallas_call x1, Pallas kernels: 78.9 us -> 77.7 us  [project(): pl.pallas_call(functools.partial(project_kernel, n_ctx, n), out_shape=jax...]
where the time goes in v6:
time: 112 us; the launch traced here: 111 us
  Pallas kernels  106 us (95%)
  local copies, waits for them, and re-layouts  3.52 us (3%)
  other arithmetic  2.06 us (2%)
    pallas_call x1, Pallas kernels, project(): pl.pallas_call(functools.partial(project_kernel, n_ctx, n), out_shape=jax...  77.7 us
    pallas_call x1, Pallas kernels, gather(): pl.pallas_call(functools.partial(gather_kernel, n, n_tp), out_shape=(jax....  20.3 us
    pallas_call x1, Pallas kernels, attention(): pl.pallas_call(attention_kernel, out_shape=(jax.ShapeDtypeStruct((tokens,...  7.77 us

profile of v6, /device:TPU:12, one launch (start us, length us, event | category | flops | bytes accessed | tf_op | source)
XLA Modules:
  0.0 111.4 jit_solution(10290417007079083918)
XLA Ops:
  0.0 0.8 dynamic_slice.3
  0.8 0.0 copy-start
  0.8 0.7 convert_element_type.10
  1.5 0.8 copy.13.segk_ref
  2.2 0.5 fusion
  2.8 0.8 pad_maximum_fusion
  3.6 20.3 %gather.1 = (bf16[8,256,512]{2,1,0:T(8,128)(2,1)}, bf16[2,2,640,128]{3,2,1,0:T(8,128)(2,1)}, bf16[2,2,640,128]{3,2,1,0:T(8,128)(2,1)}, bf16[2,2,128,640]{3,2,1,0...) custom-call(bf16[256,256]{1,0:T(8,128)(2,1)} %kp_hbm.1, ...), custom_call_target="tpu_custom_call" | custom-call | tf_op jit(solution)/shard_map/gather/pallas_call | solution.py:214
  23.9 0.0 copy-done
  23.9 7.8 %attention.1 = (bf16[256,1280]{1,0:T(8,128)(2,1)}, f32[2048,512]{1,0:T(8,128)}) custom-call(s32[1]{0:T(128)} %bitcast.start_ref, s32[16,16]{1,0:T(8,128)} %mask_ref.1, bf16[2,2,640,128]{3,2,1,0:T(8,128)(2,1)} %get-tuple-element.14.qs, bf16[2,2,640,128]{3,2,1,0:T(8,128)(2,1)} %get-tuple-element.15.dos, bf16[2,2,128,640]{3,2,1,0:T(8,128)(2,1)} %get-tuple-element.16.qt_s, ...), custom_call_target="tpu_custom_call" | custom-call | tf_op jit(solution)/shard_map/attention/pallas_call | solution.py:320
  31.7 77.7 %project.1 = bf16[1280,256]{1,0:T(8,128)(2,1)} custom-call(bf16[256,1280]{1,0:T(8,128)(2,1)} %get-tuple-element.20.dq_hbm, f32[2048,512]{1,0:T(8,128)} %get-tuple-element.21.terms_ref, f32[256,128]{1,0:T(8,128)} %get-tuple-element.26.cos_ref, f32[256,128]{1,0:T(8,128)} %get-tuple-element.27.sin_ref, bf16[5120,1280]{1,0:T(8,128)(2,1)} %wq_ref.1, ...), custom_call_target="tpu_custom_call" | custom-call | tf_op jit(solution)/shard_map/project/pallas_call | solution.py:686
  109.4 2.0 %copy.15 = bf16[1280,256]{1,0:T(8,128)(2,1)} copy(bf16[1280,256]{1,0:T(8,128)(2,1)} %project.1) | data formatting | bytes 1310720
  (1 shorter events, 0.0 us)
Async XLA Ops:
  0.8 23.1 %copy-start = (s32[256]{0:T(256)}, s32[256]{0:T(256)S(1)}, u32[]{:S(2)}) copy-start(s32[256]{0:T(256)S(1)} %dynamic_slice.3) | copy-start | bytes 3076
